TPU v7x, 32 devices: a whole 2x2x4 slice. The times are simulated.
32 devices in a mesh: dp: 16 (over z, x, core), tensor: 2 (over y).
Axes of the slice: x: 2, y: 2, z: 4, core: 2. Of those that a mesh axis runs over, the one named last changes fastest.
Arguments:
- tokens: bfloat16 [32768, 768], P(('dp', 'tensor')), may hold values from -6 to 6
- segment_ids: int32 [64, 512], P('dp'), may hold values from 0 to 3, never falling along the last dimension, each value on 1 to 256 neighbouring positions
- w_query: bfloat16 [768, 768], P('dp', 'tensor'), may hold values from -0.21875 to 0.21875
- w_key: bfloat16 [768, 768], P('dp', 'tensor'), may hold values from -0.21875 to 0.21875
- w_value: bfloat16 [768, 768], P('dp', 'tensor'), may hold values from -0.21875 to 0.21875
- w_out: bfloat16 [768, 768], P('tensor', 'dp'), may hold values from -1.75 to 1.75
- w_up: bfloat16 [768, 3072], P('dp', 'tensor'), may hold values from -0.21875 to 0.21875
- w_down: bfloat16 [3072, 768], P('tensor', 'dp'), may hold values from -0.109375 to 0.109375
- b_query: bfloat16 [768], P(('tensor', 'dp')), may hold values from -3 to 3
- b_value: bfloat16 [768], P(('tensor', 'dp')), may hold values from -3 to 3
- b_out: bfloat16 [768], P('dp'), may hold values from -3 to 3
- b_up: bfloat16 [3072], P(('tensor', 'dp')), may hold values from -3 to 3
- b_down: bfloat16 [768], P('dp'), may hold values from -3 to 3
- attn_gain: bfloat16 [768], P('dp'), may hold values from 0.099609375 to 1.8984375
- attn_shift: bfloat16 [768], P('dp'), may hold values from -3 to 3
- ffn_gain: bfloat16 [768], P('dp'), may hold values from 0.099609375 to 1.8984375
- ffn_shift: bfloat16 [768], P('dp'), may hold values from -3 to 3
- cotangent: bfloat16 [32768, 768], P(('dp', 'tensor')), may hold values from -6 to 6
Outputs:
- block_out: bfloat16 [32768, 768], P(('dp', 'tensor'))
- grad_tokens: float32 [32768, 768], P(('dp', 'tensor'))
- grad_w_query: float32 [768, 768], P('dp', 'tensor')
- grad_w_key: float32 [768, 768], P('dp', 'tensor')
- grad_w_value: float32 [768, 768], P('dp', 'tensor')
- grad_w_out: float32 [768, 768], P('tensor', 'dp')
- grad_w_up: float32 [768, 3072], P('dp', 'tensor')
- grad_w_down: float32 [3072, 768], P('tensor', 'dp')
- grad_b_query: float32 [768], P(('tensor', 'dp'))
- grad_b_value: float32 [768], P(('tensor', 'dp'))
- grad_b_out: float32 [768], P('dp')
- grad_b_up: float32 [3072], P(('tensor', 'dp'))
- grad_b_down: float32 [768], P('dp')
- grad_attn_gain: float32 [768], P('dp')
- grad_attn_shift: float32 [768], P('dp')
- grad_ffn_gain: float32 [768], P('dp')
- grad_ffn_shift: float32 [768], P('dp')
Inputs may be any that keep to these rules, and one draw needn't show every extreme that they name: `segment_ids`: along each sequence the numbers never fall; each sequence holds all 4 documents, each of one or more tokens, and no document holds more than half of 512 tokens.
All inputs are finite; a program needn't handle non-finite values.
Results may differ from a plain program's by a relative error of at most 0.023.
Values may be sent and summed in bfloat16 or wider, within the bound.
A program may use at most 128 MiB of HBM per device.

v0:
```python
import math

import jax
import jax.numpy as jnp
from jax import lax
from jax.sharding import PartitionSpec as P

HEAD = 64
SEQ = 512


norm_eps = 1e-06
masked_score = -1000000000.0
gelu_slope = 0.7978845608028654


def gelu_tanh(argument):
    return (
        0.5
        * argument
        * (1.0 + jnp.tanh(gelu_slope * (argument + 0.044715 * argument * argument * argument)))
    )


def matmul(left_rows, right_rows):
    return jnp.dot(left_rows, right_rows, preferred_element_type=jnp.float32)


def contract_rows(left_rows, right_rows):
    return lax.dot_general(
        left_rows, right_rows, (((0,), (0,)), ((), ())), preferred_element_type=jnp.float32
    )


def contract_cols(left_rows, right_rows):
    return lax.dot_general(
        left_rows, right_rows, (((1,), (1,)), ((), ())), preferred_element_type=jnp.float32
    )


def norm_forward(residual, gain_row, shift_row):
    centred = residual - jnp.mean(residual, axis=-1, keepdims=True)
    variance = jnp.mean(centred * centred, axis=-1, keepdims=True)
    inverse = lax.rsqrt(variance + norm_eps)
    normal = centred * inverse
    return (normal * gain_row + shift_row, normal, inverse)


def norm_backward(grad_rows, normal, inverse, gain_row):
    scaled = grad_rows * gain_row
    return inverse * (
        scaled
        - jnp.mean(scaled, axis=-1, keepdims=True)
        - normal * jnp.mean(scaled * normal, axis=-1, keepdims=True)
    )


def masked_scores(queries, key_rows, segments):
    scale_factor = 1.0 / math.sqrt(HEAD)
    scores = (
        jnp.einsum("qhe,khe->hqk", queries, key_rows, preferred_element_type=jnp.float32)
        * scale_factor
    )
    same_doc = segments[:, None] == segments[None, :]
    return jnp.where(same_doc[None], scores, masked_score)


def attend_forward(inputs_block):
    queries, key_rows, value_rows, segments = inputs_block
    scores = masked_scores(queries, key_rows, segments)
    row_max = jnp.max(scores, axis=-1, keepdims=True)
    unnormed = jnp.exp(scores - row_max)
    row_total = jnp.sum(unnormed, axis=-1, keepdims=True)
    softmax_rows = (unnormed / row_total).astype(jnp.bfloat16)
    mixture = jnp.einsum(
        "hqk,khe->qhe", softmax_rows, value_rows, preferred_element_type=jnp.float32
    )
    return (mixture.astype(jnp.bfloat16), (row_max + jnp.log(row_total))[..., 0])


def attend_backward(inputs_block):
    queries, key_rows, value_rows, segments, log_total, grad_mixture = inputs_block
    scores = masked_scores(queries, key_rows, segments)
    softmax_full = jnp.exp(scores - log_total[..., None])
    softmax_rows = softmax_full.astype(jnp.bfloat16)
    grad_values = jnp.einsum(
        "hqk,qhe->khe", softmax_rows, grad_mixture, preferred_element_type=jnp.float32
    )
    grad_probs = jnp.einsum(
        "qhe,khe->hqk", grad_mixture, value_rows, preferred_element_type=jnp.float32
    )
    row_dot = jnp.sum(softmax_full * grad_probs, axis=-1, keepdims=True)
    grad_scores = (softmax_full * (grad_probs - row_dot)).astype(jnp.bfloat16)
    scale_factor = 1.0 / math.sqrt(HEAD)
    grad_queries = (
        jnp.einsum("hqk,khe->qhe", grad_scores, key_rows, preferred_element_type=jnp.float32)
        * scale_factor
    )
    grad_keys = (
        jnp.einsum("hqk,qhe->khe", grad_scores, queries, preferred_element_type=jnp.float32)
        * scale_factor
    )
    return (
        grad_queries.astype(jnp.bfloat16),
        grad_keys.astype(jnp.bfloat16),
        grad_values.astype(jnp.bfloat16),
    )


def local(
    tokens,
    segment_ids,
    w_query,
    w_key,
    w_value,
    w_out,
    w_up,
    w_down,
    b_query,
    b_value,
    b_out,
    b_up,
    b_down,
    attn_gain,
    attn_shift,
    ffn_gain,
    ffn_shift,
    cotangent,
):
    query_w, key_w, value_w, out_w, query_b, value_b, out_b, gain_one, shift_one = (
        lax.all_gather(w_query, "dp", axis=0, tiled=True),
        lax.all_gather(w_key, "dp", axis=0, tiled=True),
        lax.all_gather(w_value, "dp", axis=0, tiled=True),
        lax.all_gather(w_out, "dp", axis=1, tiled=True),
        lax.all_gather(b_query, "dp", axis=0, tiled=True),
        lax.all_gather(b_value, "dp", axis=0, tiled=True),
        lax.all_gather(b_out, "dp", axis=0, tiled=True),
        lax.all_gather(attn_gain, "dp", axis=0, tiled=True),
        lax.all_gather(attn_shift, "dp", axis=0, tiled=True),
    )
    up_w, down_w, up_b, down_b, gain_two, shift_two = (
        lax.all_gather(w_up, "dp", axis=0, tiled=True),
        lax.all_gather(w_down, "dp", axis=1, tiled=True),
        lax.all_gather(b_up, "dp", axis=0, tiled=True),
        lax.all_gather(b_down, "dp", axis=0, tiled=True),
        lax.all_gather(ffn_gain, "dp", axis=0, tiled=True),
        lax.all_gather(ffn_shift, "dp", axis=0, tiled=True),
    )
    gain_one = gain_one.astype(jnp.float32)
    gain_two = gain_two.astype(jnp.float32)
    gathered = lax.all_gather(tokens, "tensor", axis=0, tiled=True)
    group_rows = gathered.shape[0]
    local_heads = query_w.shape[1] // HEAD
    seq_count = group_rows // SEQ
    head_shape = (seq_count, SEQ, local_heads, HEAD)
    queries = (matmul(gathered, query_w) + query_b.astype(jnp.float32)).astype(jnp.bfloat16)
    key_rows = matmul(gathered, key_w).astype(jnp.bfloat16)
    value_rows = (matmul(gathered, value_w) + value_b.astype(jnp.float32)).astype(jnp.bfloat16)
    mixture, log_total = lax.map(
        attend_forward,
        (
            queries.reshape(head_shape),
            key_rows.reshape(head_shape),
            value_rows.reshape(head_shape),
            segment_ids,
        ),
    )
    mixture = mixture.reshape(group_rows, local_heads * HEAD)
    attn_part = lax.psum_scatter(
        matmul(mixture, out_w).astype(jnp.bfloat16), "tensor", scatter_dimension=0, tiled=True
    ).astype(jnp.float32)
    residual_one = tokens.astype(jnp.float32) + (attn_part + out_b.astype(jnp.float32))
    norm_one, normal_one, inverse_one = norm_forward(
        residual_one, gain_one, shift_one.astype(jnp.float32)
    )
    normed = lax.all_gather(norm_one.astype(jnp.bfloat16), "tensor", axis=0, tiled=True)
    up_proj = matmul(normed, up_w) + up_b.astype(jnp.float32)
    hidden = gelu_tanh(up_proj).astype(jnp.bfloat16)
    ffn_part = lax.psum_scatter(
        matmul(hidden, down_w).astype(jnp.bfloat16), "tensor", scatter_dimension=0, tiled=True
    ).astype(jnp.float32)
    residual_two = norm_one + (ffn_part + down_b.astype(jnp.float32))
    norm_two, normal_two, inverse_two = norm_forward(
        residual_two, gain_two, shift_two.astype(jnp.float32)
    )
    block_out = norm_two.astype(jnp.bfloat16)
    grad_out = cotangent.astype(jnp.float32)
    gain_two_grad = jnp.sum(grad_out * normal_two, axis=0)
    shift_two_grad = jnp.sum(grad_out, axis=0)
    grad_two = norm_backward(grad_out, normal_two, inverse_two, gain_two)
    grad_ffn = grad_two.astype(jnp.bfloat16)
    shard_rows = lax.all_gather(grad_ffn, "tensor", axis=0, tiled=True)
    down_grad = contract_rows(hidden, shard_rows)
    hidden_grad = contract_cols(shard_rows, down_w)
    down_grad, hidden_grad = (down_grad, hidden_grad)
    gelu_value, gelu_pull = jax.vjp(gelu_tanh, up_proj)
    grad_up = gelu_pull(hidden_grad)[0].astype(jnp.bfloat16)
    up_grad_w = contract_rows(normed, grad_up)
    up_grad_b = jnp.sum(grad_up, axis=0, dtype=jnp.float32)
    grad_norm_one = grad_two + lax.psum_scatter(
        contract_cols(grad_up, up_w).astype(jnp.bfloat16), "tensor", scatter_dimension=0, tiled=True
    ).astype(jnp.float32)
    gain_one_grad = jnp.sum(grad_norm_one * normal_one, axis=0)
    shift_one_grad = jnp.sum(grad_norm_one, axis=0)
    grad_one = norm_backward(grad_norm_one, normal_one, inverse_one, gain_one)
    grad_attn = grad_one.astype(jnp.bfloat16)
    gain_one_sum, shift_one_sum, gain_two_sum, shift_two_sum, out_b_sum, down_b_sum = lax.psum(
        (
            gain_one_grad,
            shift_one_grad,
            gain_two_grad,
            shift_two_grad,
            jnp.sum(grad_attn, axis=0, dtype=jnp.float32),
            jnp.sum(grad_ffn, axis=0, dtype=jnp.float32),
        ),
        "tensor",
    )
    shard_rows = lax.all_gather(grad_attn, "tensor", axis=0, tiled=True)
    out_grad = contract_rows(mixture, shard_rows)
    mixture_grad = contract_cols(shard_rows, out_w)
    out_grad, mixture_grad = (out_grad, mixture_grad)
    grad_mixture = mixture_grad.astype(jnp.bfloat16).reshape(head_shape)
    grad_q, grad_k, grad_v = lax.map(
        attend_backward,
        (
            queries.reshape(head_shape),
            key_rows.reshape(head_shape),
            value_rows.reshape(head_shape),
            segment_ids,
            log_total,
            grad_mixture,
        ),
    )
    flat_shape = (group_rows, local_heads * HEAD)
    grad_q = grad_q.reshape(flat_shape)
    grad_k = grad_k.reshape(flat_shape)
    grad_v = grad_v.reshape(flat_shape)
    query_grad_w = contract_rows(gathered, grad_q)
    key_grad_w = contract_rows(gathered, grad_k)
    value_grad_w = contract_rows(gathered, grad_v)
    query_grad_b = jnp.sum(grad_q, axis=0, dtype=jnp.float32)
    value_grad_b = jnp.sum(grad_v, axis=0, dtype=jnp.float32)
    grad_tokens = grad_one + lax.psum_scatter(
        (
            contract_cols(grad_q, query_w)
            + contract_cols(grad_k, key_w)
            + contract_cols(grad_v, value_w)
        ).astype(jnp.bfloat16),
        "tensor",
        scatter_dimension=0,
        tiled=True,
    ).astype(jnp.float32)
    (
        sum_query_w,
        sum_key_w,
        sum_value_w,
        sum_out_w,
        sum_up_w,
        sum_down_w,
        sum_query_b,
        sum_value_b,
        sum_up_b,
        sum_out_b,
        sum_down_b,
        sum_gain_one,
        sum_shift_one,
        sum_gain_two,
        sum_shift_two,
    ) = (
        lax.psum_scatter(query_grad_w, "dp", scatter_dimension=0, tiled=True),
        lax.psum_scatter(key_grad_w, "dp", scatter_dimension=0, tiled=True),
        lax.psum_scatter(value_grad_w, "dp", scatter_dimension=0, tiled=True),
        lax.psum_scatter(out_grad, "dp", scatter_dimension=1, tiled=True),
        lax.psum_scatter(up_grad_w, "dp", scatter_dimension=0, tiled=True),
        lax.psum_scatter(down_grad, "dp", scatter_dimension=1, tiled=True),
        lax.psum_scatter(query_grad_b, "dp", scatter_dimension=0, tiled=True),
        lax.psum_scatter(value_grad_b, "dp", scatter_dimension=0, tiled=True),
        lax.psum_scatter(up_grad_b, "dp", scatter_dimension=0, tiled=True),
        lax.psum_scatter(out_b_sum, "dp", scatter_dimension=0, tiled=True),
        lax.psum_scatter(down_b_sum, "dp", scatter_dimension=0, tiled=True),
        lax.psum_scatter(gain_one_sum, "dp", scatter_dimension=0, tiled=True),
        lax.psum_scatter(shift_one_sum, "dp", scatter_dimension=0, tiled=True),
        lax.psum_scatter(gain_two_sum, "dp", scatter_dimension=0, tiled=True),
        lax.psum_scatter(shift_two_sum, "dp", scatter_dimension=0, tiled=True),
    )
    return (
        block_out,
        grad_tokens,
        sum_query_w,
        sum_key_w,
        sum_value_w,
        sum_out_w,
        sum_up_w,
        sum_down_w,
        sum_query_b,
        sum_value_b,
        sum_out_b,
        sum_up_b,
        sum_down_b,
        sum_gain_one,
        sum_shift_one,
        sum_gain_two,
        sum_shift_two,
    )


def solution(mesh):
    return jax.shard_map(
        local,
        mesh=mesh,
        in_specs=(
            P(("dp", "tensor"), None),
            P("dp", None),
            P("dp", "tensor"),
            P("dp", "tensor"),
            P("dp", "tensor"),
            P("tensor", "dp"),
            P("dp", "tensor"),
            P("tensor", "dp"),
            P(("tensor", "dp")),
            P(("tensor", "dp")),
            P("dp"),
            P(("tensor", "dp")),
            P("dp"),
            P("dp"),
            P("dp"),
            P("dp"),
            P("dp"),
            P(("dp", "tensor"), None),
        ),
        out_specs=(
            P(("dp", "tensor"), None),
            P(("dp", "tensor"), None),
            P("dp", "tensor"),
            P("dp", "tensor"),
            P("dp", "tensor"),
            P("tensor", "dp"),
            P("dp", "tensor"),
            P("tensor", "dp"),
            P(("tensor", "dp")),
            P(("tensor", "dp")),
            P("dp"),
            P(("tensor", "dp")),
            P("dp"),
            P("dp"),
            P("dp"),
            P("dp"),
            P("dp"),
        ),
        check_vma=False,
    )
```

profile of v0, /device:TPU:0, one launch (start us, length us, event | category | flops | bytes accessed | tf_op | source)
XLA Modules:
  0.0 1139.0 jit_solution(12009393150159343911)
XLA Ops:
  19.7 62.9 %all-reduce.20 = (bf16[768]{0:T(1024)(128)(2,1)S(1)}, bf16[768]{0:T(1024)(128)(2,1)S(1)}, bf16[384]{0:T(512)(128)(2,1)S(1)}, bf16[384]{0:T(512)(128)(2,1)S(1)}, ...) all-reduce(bf16[768]{0:T(1024)(128)(2,1)S(1)} %dynamic-update-slice, ...), channel_id=1, replica_groups=mesh['dp'=16,'tensor'=2] {'dp'}, use_global_device_ids=true, to_apply=%add.4 | all-reduce | flops 6912 | bytes 27648
  82.7 20.5 %all_gather.60 = bf16[768,384]{1,0:T(8,128)(2,1)} all-gather(bf16[48,384]{1,0:T(8,128)(2,1)} %param.24), channel_id=1, replica_groups=mesh['dp'=16,'tensor'=2] {'dp'}, dimensions={0}, use_global_device_ids=true | all-gather | bytes 626688 | tf_op jit(solution)/shard_map/all_gather | solution.py:131
  103.2 22.3 %all_gather.62 = bf16[768,384]{1,0:T(8,128)(2,1)} all-gather(bf16[48,384]{1,0:T(8,128)(2,1)} %param.25), channel_id=1, replica_groups=mesh['dp'=16,'tensor'=2] {'dp'}, dimensions={0}, use_global_device_ids=true | all-gather | bytes 626688 | tf_op jit(solution)/shard_map/all_gather | solution.py:132
  125.5 19.3 %all_gather.58 = bf16[768,384]{1,0:T(8,128)(2,1)S(1)} all-gather(bf16[48,384]{1,0:T(8,128)(2,1)} %param.26), channel_id=1, replica_groups=mesh['dp'=16,'tensor'=2] {'dp'}, dimensions={0}, use_global_device_ids=true | all-gather | bytes 626688 | tf_op jit(solution)/shard_map/all_gather | solution.py:133
  144.8 21.7 %all_gather.63 = bf16[384,768]{0,1:T(8,128)(2,1)} all-gather(bf16[384,48]{0,1:T(8,128)(2,1)S(1)} %copy-done.19), channel_id=1, replica_groups=mesh['dp'=16,'tensor'=2] {'dp'}, dimensions={1}, use_global_device_ids=true | all-gather | bytes 626688 | tf_op jit(solution)/shard_map/all_gather | solution.py:134
  166.5 3.7 add_convert_fusion.3
  173.9 3.7 add_convert_fusion.2
  180.6 4.8 convolution_convert_fusion.4
  192.6 27.2 %while.26 = (s32[]{:T(128)}, bf16[4,512,6,64]{1,3,2,0:T(8,128)(2,1)S(1)}, f32[4,6,512]{2,1,0:T(8,128)S(1)}, bf16[4,512,6,64]{1,3,2,0:T(8,128)(2,1)}, s32[4,512]{...) while((s32[]{:T(128)}, ...), condition=%wide.region_3.4_spmd, body=%wide.region_0.3_spmd.sunk | while | flops 421983232 | bytes 21622884 | solution.py:159
  222.7 3.5 convolution_convert_fusion
  226.8 40.2 %reduce-scatter.17.cloned.1.call-done = bf16[1024,768]{1,0:T(8,128)(2,1)} async-done(((bf16[2048,768]{1,0:T(8,128)(2,1)}), bf16[1024,768]{1,0:T(8,128)(2,1)}) %reduce-scatter.17.cloned.1.call-update) | async-done | bytes 1572880 | tf_op jit(solution)/shard_map/reduce_scatter | solution.py:169
  272.7 44.2 %all-gather.9.cloned.1.call-done = bf16[2048,768]{1,0:T(8,128)(2,1)} async-done(((bf16[1024,768]{1,0:T(8,128)(2,1)}), bf16[2048,768]{1,0:T(8,128)(2,1)}) %all-gather.9.cloned.1.call-update) | async-done | bytes 3145744 | tf_op jit(solution)/shard_map/all_gather | solution.py:176
  316.9 13.7 %multiply_convert_fusion.1 = (bf16[2048,1536]{1,0:T(8,128)(2,1)}, f32[2048,1536]{1,0:T(8,128)}) fusion(f32[1536]{0:T(1024)S(1)} %convert_element_type.149, bf16[2048,768]{1,0:T(8,128)(2,1)} %all-gather.9.cloned.1.call-done, bf16[768,1536]{1,0:T(8,128)(2,1)} %all-gather.11.cloned.1.call-done), kind=kOutput, calls=%fused_computation.77 | convolution fusion | flops 4863295488 | bytes 24385536 | tf_op jit(solution)/shard_map/dot_general | solution.py:26
  330.7 31.4 %all-gather.13.cloned.1.call-done = bf16[1536,768]{0,1:T(8,128)(2,1)} async-done(((bf16[1536,48]{0,1:T(8,128)(2,1)}), bf16[1536,768]{0,1:T(8,128)(2,1)}) %all-gather.13.cloned.1.call-update) | async-done | bytes 2359312 | tf_op jit(solution)/shard_map/all_gather | solution.py:143
  362.1 9.0 convolution_convert_fusion.2
  371.2 41.9 %reduce-scatter.19.cloned.1.call-done = bf16[1024,768]{1,0:T(8,128)(2,1)} async-done(((bf16[2048,768]{1,0:T(8,128)(2,1)}), bf16[1024,768]{1,0:T(8,128)(2,1)}) %reduce-scatter.19.cloned.1.call-update) | async-done | bytes 1572880 | tf_op jit(solution)/shard_map/reduce_scatter | solution.py:179
  420.2 4.0 convert_reduce_fusion.2
  424.2 44.8 %all-gather.15.cloned.1.call-done = bf16[2048,768]{1,0:T(8,128)(2,1)} async-done(((bf16[1024,768]{1,0:T(8,128)(2,1)}), bf16[2048,768]{1,0:T(8,128)(2,1)}) %all-gather.15.cloned.1.call-update) | async-done | bytes 3145744 | tf_op jit(solution)/shard_map/all_gather | solution.py:192
  469.1 18.8 %convert_reduce_fusion = (f32[1536]{0:T(1024)S(1)}, bf16[2048,1536]{1,0:T(8,128)(2,1)S(1)}) fusion(bf16[2048,768]{1,0:T(8,128)(2,1)} %all-gather.15.cloned.1.call-done, bf16[1536,768]{0,1:T(8,128)(2,1)} %all-gather.13.cloned.1.call-done, f32[2048,1536]{1,0:T(8,128)} %get-tuple-element.298, f32[1536]{0:T(1024)S(1)} %convert_element_type.149), kind=kOutput, calls=%fused_computation.76 | convolution fusion | flops 4916771328 | bytes 24391680 | tf_op jit(solution)/shard_map/dot_general | solution.py:36
  490.6 6.5 convolution_convert_fusion.1
  497.1 43.3 %reduce-scatter.21.cloned.1.call-done = bf16[1024,768]{1,0:T(8,128)(2,1)} async-done(((bf16[2048,768]{1,0:T(8,128)(2,1)}), bf16[1024,768]{1,0:T(8,128)(2,1)}) %reduce-scatter.21.cloned.1.call-update) | async-done | bytes 1572880 | tf_op jit(solution)/shard_map/reduce_scatter | solution.py:200
  540.5 3.9 multiply_reduce_fusion.1
  547.8 44.9 %all-gather.17.cloned.1.call-done = bf16[2048,768]{1,0:T(8,128)(2,1)} async-done(((bf16[1024,768]{1,0:T(8,128)(2,1)}), bf16[2048,768]{1,0:T(8,128)(2,1)}) %all-gather.17.cloned.1.call-update) | async-done | bytes 3145744 | tf_op jit(solution)/shard_map/all_gather | solution.py:218
  592.6 3.8 convolution_convert_fusion.3
  604.0 61.5 %while.27 = (s32[]{:T(128)}, bf16[4,512,6,64]{1,3,2,0:T(8,128)(2,1)}, bf16[4,512,6,64]{1,3,2,0:T(8,128)(2,1)}, bf16[4,512,6,64]{1,3,2,0:T(8,128)(2,1)}, bf16[4,5...) while((s32[]{:T(128)}, ...), condition=%wide.region_17.18_spmd, body=%wide.region_15.17_spmd.sunk | while | flops 1031468032 | bytes 52264060 | solution.py:223
  606.2 3.6 fusion.152
  609.8 3.3 multiply_reduce_fusion.7
  621.6 3.5 fusion.152
  625.1 3.3 multiply_reduce_fusion.7
  636.9 3.5 fusion.152
  640.4 3.3 multiply_reduce_fusion.7
  652.2 3.5 fusion.152
  655.8 3.3 multiply_reduce_fusion.7
  679.0 3.6 add_convert_fusion
  682.7 10.3 fusion.82
  693.1 9.8 fusion.81
  702.9 5.2 fusion.80
  708.2 4.4 convolution_bitcast_fusion.2
  715.5 4.3 convolution_bitcast_fusion
  722.6 4.3 convolution_bitcast_fusion.1
  735.2 62.2 %all-reduce.18 = (f32[384]{0:T(512)S(1)}, f32[384]{0:T(512)S(1)}, f32[768]{0:T(1024)S(1)}, f32[1536]{0:T(1024)S(1)}, f32[768]{0:T(1024)S(1)}, /*index=5*/f32[768...) all-reduce(f32[384]{0:T(512)S(1)} %reduce_sum.184, ...), channel_id=12, replica_groups=mesh['dp'=16,'tensor'=2] {'dp'}, use_global_device_ids=true, to_apply=%region_26.27.clone | all-reduce | flops 6912 | bytes 55296
  799.6 5.4 all-reduce.19
  805.0 3.4 convert_add_fusion
  808.4 77.6 %reduce-scatter.27.cloned.1.call-done = f32[48,1536]{1,0:T(8,128)} async-done(((f32[768,1536]{1,0:T(8,128)}), f32[48,1536]{1,0:T(8,128)}) %reduce-scatter.27.cloned.1.call-update) | async-done | bytes 294928 | tf_op jit(solution)/shard_map/reduce_scatter | solution.py:274
  886.0 61.4 %reduce-scatter.25.cloned.1.call-done = f32[384,48]{0,1:T(8,128)} async-done(((f32[384,768]{0,1:T(8,128)}), f32[384,48]{0,1:T(8,128)}) %reduce-scatter.25.cloned.1.call-update) | async-done | bytes 73744 | tf_op jit(solution)/shard_map/reduce_scatter | solution.py:273
  947.4 61.3 %reduce-scatter.31.cloned.1.call-done = f32[48,384]{1,0:T(8,128)} async-done(((f32[768,384]{1,0:T(8,128)}), f32[48,384]{1,0:T(8,128)}) %reduce-scatter.31.cloned.1.call-update) | async-done | bytes 73744
  1008.7 61.1 %reduce-scatter.35.cloned.1.call-done = f32[48,384]{1,0:T(8,128)} async-done(((f32[768,384]{1,0:T(8,128)}), f32[48,384]{1,0:T(8,128)}) %reduce-scatter.35.cloned.1.call-update) | async-done | bytes 73744
  1069.9 61.4 %reduce-scatter.33.cloned.1.call-done = f32[48,384]{1,0:T(8,128)} async-done(((f32[768,384]{1,0:T(8,128)}), f32[48,384]{1,0:T(8,128)}) %reduce-scatter.33.cloned.1.call-update) | async-done | bytes 73744
  (223 shorter events, 141.5 us)
Async XLA Ops:
  8.0 136.8 %copy-start.19 = (bf16[384,48]{0,1:T(8,128)(2,1)S(1)}, bf16[384,48]{0,1:T(8,128)(2,1)}, u32[]{:S(2)}) copy-start(bf16[384,48]{0,1:T(8,128)(2,1)} %param.27) | copy-start | bytes 110596
  8.0 158.5 %all-gather.7.cloned.1.call-start = ((), (), s32[]{:S(2)}) async-start(), calls=%async_computation.10 | async-start | bytes 4718592 | tf_op jit(solution)/shard_map/all_gather | solution.py:151
  8.8 258.2 %reduce-scatter.17.cloned.1.call-start = ((), (), s32[]{:S(2)}) async-start(), calls=%async_computation.11 | async-start | bytes 4718592 | tf_op jit(solution)/shard_map/reduce_scatter | solution.py:169
  144.8 21.7 %copy-start.12 = (bf16[768,384]{1,0:T(8,128)(2,1)}, bf16[768,384]{1,0:T(8,128)(2,1)S(1)}, u32[]{:S(2)}) copy-start(bf16[768,384]{1,0:T(8,128)(2,1)S(1)} %all_gather.58) | copy-start | bytes 1769476
  172.4 1.5 copy-start.10
  179.5 1.1 copy-start.14
  189.5 3.1 copy-start.18
  219.8 1.7 copy-start.2
  219.8 2.8 copy-start.17
  221.5 1.1 copy-start.16
  226.2 40.8 %copy-start = (bf16[1024,768]{1,0:T(8,128)(2,1)S(1)}, bf16[1024,768]{1,0:T(8,128)(2,1)}, u32[]{:S(2)}) copy-start(bf16[1024,768]{1,0:T(8,128)(2,1)} %param.22) | copy-start | bytes 4718596
  226.2 46.5 %all-gather.11.cloned.1.call-start = ((), (), s32[]{:S(2)}) async-start(), calls=%async_computation.13 | async-start | bytes 2506752 | tf_op jit(solution)/shard_map/all_gather | solution.py:142
  226.8 90.2 %all-gather.9.cloned.1.call-start = ((), (), s32[]{:S(2)}) async-start(), calls=%async_computation.12 | async-start | bytes 4718592 | tf_op jit(solution)/shard_map/all_gather | solution.py:176
  267.0 2.1 copy-start.1
  272.0 90.0 %all-gather.13.cloned.1.call-start = ((), (), s32[]{:S(2)}) async-start(), calls=%async_computation.14 | async-start | bytes 2506752 | tf_op jit(solution)/shard_map/all_gather | solution.py:143
  272.6 140.6 %reduce-scatter.19.cloned.1.call-start = ((), (), s32[]{:S(2)}) async-start(), calls=%async_computation.15 | async-start | bytes 4718592 | tf_op jit(solution)/shard_map/reduce_scatter | solution.py:179
  371.2 97.9 %all-gather.15.cloned.1.call-start = ((), (), s32[]{:S(2)}) async-start(), calls=%async_computation.16 | async-start | bytes 4718592 | tf_op jit(solution)/shard_map/all_gather | solution.py:192
  416.4 1.4 copy-start.9
  424.2 116.3 %reduce-scatter.21.cloned.1.call-start = ((), (), s32[]{:S(2)}) async-start(), calls=%async_computation.17 | async-start | bytes 4718592 | tf_op jit(solution)/shard_map/reduce_scatter | solution.py:200
  469.1 21.5 %copy-start.23 = (bf16[768,1536]{1,0:T(8,128)(2,1)S(1)}, bf16[768,1536]{1,0:T(8,128)(2,1)}, u32[]{:S(2)}) copy-start(bf16[768,1536]{1,0:T(8,128)(2,1)} %all-gather.11.cloned.1.call-done) | copy-start | bytes 7077892
  487.9 2.7 copy-start.24
  497.1 95.5 %all-gather.17.cloned.1.call-start = ((), (), s32[]{:S(2)}) async-start(), calls=%async_computation.18 | async-start | bytes 4718592 | tf_op jit(solution)/shard_map/all_gather | solution.py:218
  540.4 3.9 copy-start.4
  540.5 3.9 copy-start.8
  547.6 257.5 %reduce-scatter.23.cloned.1.call-start = ((), (), s32[]{:S(2)}) async-start(), calls=%async_computation.19 | async-start | bytes 4718592 | tf_op jit(solution)/shard_map/reduce_scatter | solution.py:243
  599.9 4.0 copy-start.3
  671.6 7.4 copy-start.6
  671.6 3.7 copy-start.15
  675.2 1.9 copy-start.11
  677.1 1.9 copy-start.13
  682.6 125.8 %reduce-scatter.29.cloned.1.call-start = ((), (), s32[]{:S(2)}) async-start(), calls=%async_computation.22 | async-start | bytes 5013504 | tf_op jit(solution)/shard_map/reduce_scatter | solution.py:275
  693.0 193.0 %reduce-scatter.27.cloned.1.call-start = ((), (), s32[]{:S(2)}) async-start(), calls=%async_computation.21 | async-start | bytes 5013504 | tf_op jit(solution)/shard_map/reduce_scatter | solution.py:274
  702.9 244.6 %reduce-scatter.25.cloned.1.call-start = ((), (), s32[]{:S(2)}) async-start(), calls=%async_computation.20 | async-start | bytes 1253376 | tf_op jit(solution)/shard_map/reduce_scatter | solution.py:273
  708.1 300.6 %reduce-scatter.31.cloned.1.call-start = ((), (), s32[]{:S(2)}) async-start(), calls=%async_computation.23 | async-start | bytes 1253376
  712.6 2.9 copy-start.7
  715.5 354.4 %reduce-scatter.35.cloned.1.call-start = ((), (), s32[]{:S(2)}) async-start(), calls=%async_computation.25 | async-start | bytes 1253376
  722.5 408.7 %reduce-scatter.33.cloned.1.call-start = ((), (), s32[]{:S(2)}) async-start(), calls=%async_computation.24 | async-start | bytes 1253376
  726.9 8.3 copy-start.20
  726.9 8.3 copy-start.21
  726.9 8.3 copy-start.22
  726.9 78.1 %copy-start.5 = (f32[1024,768]{1,0:T(8,128)S(1)}, f32[1024,768]{1,0:T(8,128)}, u32[]{:S(2)}) copy-start(f32[1024,768]{1,0:T(8,128)} %get-tuple-element.287) | copy-start | bytes 9437188
Sparse Core Ops, SparseCore 0:
  10.4 47.6 all-gather.6
  226.3 40.6 reduce-scatter.16
  371.3 41.8 reduce-scatter.18
  547.7 44.9 all-gather.16
  682.7 43.3 reduce-scatter.22
  730.4 75.7 reduce-scatter.28
  811.1 74.8 reduce-scatter.26
  890.2 57.1 reduce-scatter.24
  951.6 57.0 reduce-scatter.30
  1012.8 57.0 reduce-scatter.34
  1074.1 57.1 reduce-scatter.32
Sparse Core Ops, SparseCore 1:
  229.2 39.8 all-gather.10
  272.1 44.7 all-gather.8
  319.4 42.7 all-gather.12
  424.3 44.7 all-gather.14
  497.2 43.2 reduce-scatter.20
where the time goes:
time: 1140 us
  waiting for transfers between devices  616 us (54%)
  blocking collectives  214 us (19%)
  matrix products  186 us (16%)
  local copies, waits for them, and re-layouts  57 us (5%)
  other arithmetic  43.7 us (4%)
  between operations  20.5 us (2%)
    unnamed x19, waiting for transfers between devices  186 us
    unnamed x2, blocking collectives  125 us
    reduce_scatter x1, waiting for transfers between devices, local(): lax.psum_scatter(up_grad_w, 'dp', scatter_dimension=0, tiled=True)  77.6 us
    reduce_scatter x1, waiting for transfers between devices, local(): lax.psum_scatter(out_grad, 'dp', scatter_dimension=1, tiled=True)  61.4 us
    all_gather x1, waiting for transfers between devices, local(): shard_rows = lax.all_gather(grad_attn, 'tensor', axis=0, tiled=True)  44.9 us
    all_gather x1, waiting for transfers between devices, local(): shard_rows = lax.all_gather(grad_ffn, 'tensor', axis=0, tiled=True)  44.8 us
    all_gather x1, waiting for transfers between devices, local(): lax.all_gather(norm_one.astype(jnp.bfloat16), 'tensor', axis=0, tiled=True)  44.2 us
    reduce_scatter x1, waiting for transfers between devices, local(): lax.psum_scatter(contract_cols(grad_up, up_w).astype(jnp.bfloat16), 'tens...  43.3 us
  transfers between devices with their start and end apart: 16, of which 12 were waited for; matrix products, arithmetic and copies ran while one was open for 7% of the time, Pallas kernels for 0%

commit v1 on v0

v1 whole, which is shorter than its diff:
```python
import functools
import math

import jax
import jax.numpy as jnp
from jax import lax
from jax.experimental import pallas as pl
from jax.experimental.pallas import tpu as pltpu
from jax.sharding import PartitionSpec as P

HEAD = 64
SEQ = 512


norm_eps = 1e-06
masked_score = -1000000000.0
gelu_slope = 0.7978845608028654


def gelu_tanh(argument):
    return (
        0.5
        * argument
        * (1.0 + jnp.tanh(gelu_slope * (argument + 0.044715 * argument * argument * argument)))
    )


def matmul(left_rows, right_rows):
    return jnp.dot(left_rows, right_rows, preferred_element_type=jnp.float32)


def contract_rows(left_rows, right_rows):
    return lax.dot_general(
        left_rows, right_rows, (((0,), (0,)), ((), ())), preferred_element_type=jnp.float32
    )


def contract_cols(left_rows, right_rows):
    return lax.dot_general(
        left_rows, right_rows, (((1,), (1,)), ((), ())), preferred_element_type=jnp.float32
    )


def norm_forward(residual, gain_row, shift_row):
    centred = residual - jnp.mean(residual, axis=-1, keepdims=True)
    variance = jnp.mean(centred * centred, axis=-1, keepdims=True)
    inverse = lax.rsqrt(variance + norm_eps)
    normal = centred * inverse
    return (normal * gain_row + shift_row, normal, inverse)


def norm_backward(grad_rows, normal, inverse, gain_row):
    scaled = grad_rows * gain_row
    return inverse * (
        scaled
        - jnp.mean(scaled, axis=-1, keepdims=True)
        - normal * jnp.mean(scaled * normal, axis=-1, keepdims=True)
    )


MESH = pl.DeviceIdType.MESH
AUX = 128
KERNEL_VMEM = 56 * 1024 * 1024
GATHER_ORDERS = ((1, 2, 3, 0, 4), (1, 2, 0, 3, 4))
REDUCE_ORDERS = tuple(tuple(reversed(order)) for order in GATHER_ORDERS)


def place_bits():
    dp = lax.axis_index("dp")
    return (lax.axis_index("tensor"), dp // 8, (dp // 4) % 2, (dp // 2) % 2, dp % 2)


def partner(bits, axis):
    flipped = [1 - bit if index == axis else bit for index, bit in enumerate(bits)]
    tensor, *dp_bits = flipped
    return (dp_bits[0] * 8 + dp_bits[1] * 4 + dp_bits[2] * 2 + dp_bits[3], tensor)


def meet_partners(bits):
    barrier = pltpu.get_barrier_semaphore()
    for axis in range(5):
        pl.semaphore_signal(barrier, inc=1, device_id=partner(bits, axis), device_id_type=MESH)
    pl.semaphore_wait(barrier, 5)


def column_halves(columns):
    first = (columns // 256) * 128 + (128 if (columns // 128) % 2 else 0)
    return (pl.ds(0, first), pl.ds(first, columns - first)), (first, columns - first)


def gather_kernel(own_ref, all_ref, local_sem, send_sem, recv_sem):
    bits = place_bits()
    halves, _ = column_halves(own_ref.shape[-1])
    keep = pltpu.make_async_copy(own_ref, all_ref.at[tuple(bits)], local_sem)
    keep.start()
    meet_partners(bits)
    keep.wait()
    pending = [None, None]
    for step in range(5):
        for half, order in enumerate(GATHER_ORDERS):
            if pending[half] is not None:
                pending[half].wait()
            done, axis = order[:step], order[step]
            held = tuple(slice(None) if index in done else bits[index] for index in range(5))
            block = all_ref.at[held + (slice(None), halves[half])]
            pending[half] = pltpu.make_async_remote_copy(
                src_ref=block,
                dst_ref=block,
                send_sem=send_sem.at[half, step],
                recv_sem=recv_sem.at[half, step],
                device_id=partner(bits, axis),
                device_id_type=MESH,
            )
            pending[half].start()
    for copy in pending:
        copy.wait()


def gather_blocks(own):
    rows, columns = own.shape
    return pl.pallas_call(
        gather_kernel,
        out_shape=jax.ShapeDtypeStruct((2, 2, 2, 2, 2, rows, columns), own.dtype),
        in_specs=[pl.BlockSpec(memory_space=pl.ANY)],
        out_specs=pl.BlockSpec(memory_space=pl.ANY),
        scratch_shapes=[
            pltpu.SemaphoreType.DMA,
            pltpu.SemaphoreType.DMA((2, 5)),
            pltpu.SemaphoreType.DMA((2, 5)),
        ],
        compiler_params=pltpu.CompilerParams(collective_id=0, has_side_effects=True),
    )(own)


def add_received(bits, order, step, halves, half, own, received):
    gone = order[: step + 1]
    open_axes = [index for index in range(5) if index not in gone and index != 4]
    slices = own.shape[-2] // 16

    def one(index, carry):
        row = pl.ds(pl.multiple_of((index % slices) * 16, 16), 16)
        code = index // slices
        place, spot = list(bits[:4]), []
        for weight, axis in enumerate(open_axes):
            place[axis] = (code // (2**weight)) % 2
            spot.append(place[axis])
        target = tuple(place) + (row, halves[half])
        total = own[target].astype(jnp.float32) + received[tuple(spot) + (row,)].astype(jnp.float32)
        own[target] = total.astype(own.dtype)
        return carry

    lax.fori_loop(0, slices * 2 ** len(open_axes), one, 0)


def reduce_kernel(parts_ref, sum_ref, own, *scratch):
    received = (scratch[:5], scratch[5:10])
    local_sem, send_sem, recv_sem = scratch[10:]
    bits = place_bits()
    halves, _ = column_halves(own.shape[-1])
    everything = slice(None)
    keep = pltpu.make_async_copy(parts_ref.at[(everything,) * 4 + (bits[4],)], own, local_sem)
    keep.start()
    meet_partners(bits)

    def copy_of(half, step):
        order = REDUCE_ORDERS[half]
        axis = order[step]
        if step == 0:
            block = parts_ref.at[
                (everything,) * 4 + (1 - bits[4], everything, halves[half])
            ]
        else:
            place = tuple(
                1 - bits[index]
                if index == axis
                else (bits[index] if index in order[:step] else everything)
                for index in range(4)
            )
            block = own.at[place + (everything, halves[half])]
        return pltpu.make_async_remote_copy(
            src_ref=block,
            dst_ref=received[half][step],
            send_sem=send_sem.at[half, step],
            recv_sem=recv_sem.at[half, step],
            device_id=partner(bits, axis),
            device_id_type=MESH,
        )

    pending = [copy_of(half, 0) for half in range(2)]
    for copy in pending:
        copy.start()
    keep.wait()
    for step in range(5):
        for half in range(2):
            pending[half].wait()
            if step < 4:
                add_received(
                    bits, REDUCE_ORDERS[half], step, halves, half, own, received[half][step]
                )
                pending[half] = copy_of(half, step + 1)
                pending[half].start()
            else:
                sum_ref[:, halves[half]] = own[tuple(bits[:4]) + (everything, halves[half])].astype(
                    jnp.float32
                ) + received[half][4][...].astype(jnp.float32)


def reduce_blocks(parts):
    rows, columns = parts.shape[-2:]
    _, widths = column_halves(columns)
    return pl.pallas_call(
        reduce_kernel,
        out_shape=jax.ShapeDtypeStruct((rows, columns), jnp.float32),
        in_specs=[pl.BlockSpec(memory_space=pl.ANY)],
        out_specs=pl.BlockSpec(memory_space=pltpu.VMEM),
        scratch_shapes=[pltpu.VMEM((2, 2, 2, 2, rows, columns), parts.dtype)]
        + [
            pltpu.VMEM((2,) * (4 - step) + (rows, width), parts.dtype)
            for width in widths
            for step in range(5)
        ]
        + [
            pltpu.SemaphoreType.DMA,
            pltpu.SemaphoreType.DMA((2, 5)),
            pltpu.SemaphoreType.DMA((2, 5)),
        ],
        compiler_params=pltpu.CompilerParams(
            collective_id=1, has_side_effects=True, vmem_limit_bytes=KERNEL_VMEM
        ),
    )(parts)


def head_scores(query_block, keys, same_doc, lanes, head):
    masked = jnp.where(lanes == head, query_block, jnp.zeros_like(query_block))
    scores = contract_cols(masked, keys) * (1.0 / math.sqrt(HEAD))
    return jnp.where(same_doc, scores, masked_score)


def attend_forward_kernel(q_ref, k_ref, v_ref, seg_row_ref, seg_col_ref, mix_ref, log_ref):
    queries, keys, values = q_ref[0], k_ref[0], v_ref[0]
    same_doc = seg_col_ref[0] == seg_row_ref[0]
    lanes = lax.broadcasted_iota(jnp.int32, queries.shape, 1) // HEAD
    results = []
    for head in range(2):
        scores = head_scores(queries, keys, same_doc, lanes, head)
        row_max = jnp.max(scores, axis=-1, keepdims=True)
        unnormed = jnp.exp(scores - row_max)
        row_total = jnp.sum(unnormed, axis=-1, keepdims=True)
        mixed = matmul(unnormed.astype(jnp.bfloat16), values) * (1.0 / row_total)
        results.append((mixed, row_max + jnp.log(row_total)))
    mix_ref[0] = jnp.where(lanes == 0, results[0][0], results[1][0]).astype(jnp.bfloat16)
    log_ref[0] = jnp.where(lanes == 0, results[0][1], results[1][1])


def attend_backward_kernel(
    q_ref, k_ref, v_ref, seg_row_ref, seg_col_ref, log_ref, g_ref, dq_ref, dk_ref, dv_ref
):
    queries, keys, values, grads = q_ref[0], k_ref[0], v_ref[0], g_ref[0]
    same_doc = seg_col_ref[0] == seg_row_ref[0]
    lanes = lax.broadcasted_iota(jnp.int32, queries.shape, 1) // HEAD
    scale_factor = 1.0 / math.sqrt(HEAD)
    results = []
    for head in range(2):
        scores = head_scores(queries, keys, same_doc, lanes, head)
        softmax_full = jnp.exp(scores - log_ref[0][:, head * HEAD : head * HEAD + 1])
        grad_values = contract_rows(softmax_full.astype(jnp.bfloat16), grads)
        grad_probs = contract_cols(jnp.where(lanes == head, grads, jnp.zeros_like(grads)), values)
        row_dot = jnp.sum(softmax_full * grad_probs, axis=-1, keepdims=True)
        grad_scores = (softmax_full * (grad_probs - row_dot)).astype(jnp.bfloat16)
        results.append(
            (
                matmul(grad_scores, keys) * scale_factor,
                contract_rows(grad_scores, queries) * scale_factor,
                grad_values,
            )
        )
    for ref, first, second in zip((dq_ref, dk_ref, dv_ref), results[0], results[1]):
        ref[0] = jnp.where(lanes == 0, first, second).astype(jnp.bfloat16)


def head_block(offset):
    return pl.BlockSpec((1, SEQ, 2 * HEAD), lambda g, s, p: (g, s, p + offset))


def attention_specs(pairs):
    return [
        head_block(0),
        head_block(pairs),
        head_block(2 * pairs),
        pl.BlockSpec((1, 1, SEQ), lambda g, s, p: (s, 0, 0)),
        pl.BlockSpec((1, SEQ, 1), lambda g, s, p: (s, 0, 0)),
    ]


def attend_forward(qkv, seg_row, seg_col):
    groups, rows, columns = qkv.shape
    pairs = columns // (6 * HEAD)
    return pl.pallas_call(
        attend_forward_kernel,
        grid=(groups, rows // SEQ, pairs),
        in_specs=attention_specs(pairs),
        out_specs=[head_block(0), head_block(0)],
        out_shape=[
            jax.ShapeDtypeStruct((groups, rows, columns // 3), jnp.bfloat16),
            jax.ShapeDtypeStruct((groups, rows, columns // 3), jnp.float32),
        ],
        compiler_params=pltpu.CompilerParams(vmem_limit_bytes=KERNEL_VMEM),
    )(qkv, qkv, qkv, seg_row, seg_col)


def attend_backward(qkv, seg_row, seg_col, log_total, grad_mixture):
    groups, rows, columns = qkv.shape
    pairs = columns // (6 * HEAD)
    return pl.pallas_call(
        attend_backward_kernel,
        grid=(groups, rows // SEQ, pairs),
        in_specs=attention_specs(pairs) + [head_block(0), head_block(0)],
        out_specs=[head_block(0)] * 3,
        out_shape=[jax.ShapeDtypeStruct((groups, rows, columns // 3), jnp.bfloat16)] * 3,
        compiler_params=pltpu.CompilerParams(vmem_limit_bytes=KERNEL_VMEM),
    )(qkv, qkv, qkv, seg_row, seg_col, log_total, grad_mixture)


def local(
    groups,
    dp_size,
    tokens,
    segment_ids,
    w_query,
    w_key,
    w_value,
    w_out,
    w_up,
    w_down,
    b_query,
    b_value,
    b_out,
    b_up,
    b_down,
    attn_gain,
    attn_shift,
    ffn_gain,
    ffn_shift,
    cotangent,
):
    rows, heads_width = w_query.shape
    units = w_up.shape[1]
    half = b_query.shape[0]
    lines = b_up.shape[0] // rows
    kernels = rows % 16 == 0 and dp_size == 16 and groups == 2
    pad_half = (0, rows - half)
    aux = jnp.stack(
        [b_out, b_down, attn_gain, attn_shift, ffn_gain, ffn_shift]
        + [jnp.pad(b_query, pad_half), jnp.pad(b_value, pad_half)]
        + [b_up[line * rows : (line + 1) * rows] for line in range(lines)],
        axis=1,
    )
    aux = jnp.pad(aux, ((0, 0), (0, AUX - aux.shape[1])))
    own = jnp.concatenate([w_query, w_key, w_value, w_out.T, w_up, w_down.T, aux], axis=1)
    columns = own.shape[1]
    if kernels:
        every = gather_blocks(own)
    else:
        every = lax.all_gather(own, ("tensor", "dp"), axis=0, tiled=False)
    every = every.reshape(groups, dp_size * rows, columns)
    at_out = 3 * heads_width
    at_up = at_out + heads_width
    at_down = at_up + units
    at_aux = at_down + units
    qkv_w = every[:, :, :at_out]
    out_w = every[:, :, at_out:at_up]
    up_w = every[:, :, at_up:at_down]
    down_w = every[:, :, at_down:at_aux]
    small = every[:, :, at_aux:].astype(jnp.float32)
    whole = [small[0, :, index] for index in range(6)]
    out_b, down_b, gain_one, shift_one, gain_two, shift_two = whole
    by_device = small.reshape(groups, dp_size, rows, AUX)
    query_b = by_device[:, :, :half, 6].reshape(groups, heads_width)
    value_b = by_device[:, :, :half, 7].reshape(groups, heads_width)
    up_b = jnp.moveaxis(by_device[:, :, :, 8 : 8 + lines], 3, 2).reshape(groups, units)
    qkv_b = jnp.concatenate([query_b, jnp.zeros_like(query_b), value_b], axis=1)

    seq_count = tokens.shape[0] // SEQ
    segments = lax.dynamic_slice_in_dim(
        segment_ids, lax.axis_index("tensor") * seq_count, seq_count, axis=0
    )
    seg_row, seg_col = segments[:, None, :], segments[:, :, None]
    qkv = jnp.stack(
        [(matmul(tokens, qkv_w[g]) + qkv_b[g]).astype(jnp.bfloat16) for g in range(groups)]
    )
    mixture, log_total = attend_forward(qkv, seg_row, seg_col)
    attn_part = sum(contract_cols(mixture[g], out_w[g]) for g in range(groups))
    residual_one = tokens.astype(jnp.float32) + (attn_part + out_b)
    norm_one, normal_one, inverse_one = norm_forward(residual_one, gain_one, shift_one)
    normed = norm_one.astype(jnp.bfloat16)
    up_proj = [matmul(normed, up_w[g]) + up_b[g] for g in range(groups)]
    hidden = [gelu_tanh(up_proj[g]).astype(jnp.bfloat16) for g in range(groups)]
    ffn_part = sum(contract_cols(hidden[g], down_w[g]) for g in range(groups))
    residual_two = norm_one + (ffn_part + down_b)
    norm_two, normal_two, inverse_two = norm_forward(residual_two, gain_two, shift_two)
    block_out = norm_two.astype(jnp.bfloat16)

    grad_out = cotangent.astype(jnp.float32)
    gain_two_grad = jnp.sum(grad_out * normal_two, axis=0)
    shift_two_grad = jnp.sum(grad_out, axis=0)
    grad_two = norm_backward(grad_out, normal_two, inverse_two, gain_two)
    grad_ffn = grad_two.astype(jnp.bfloat16)
    down_b_grad = jnp.sum(grad_ffn, axis=0, dtype=jnp.float32)
    down_grad = [contract_rows(grad_ffn, hidden[g]) for g in range(groups)]
    grad_up = []
    for g in range(groups):
        _, gelu_pull = jax.vjp(gelu_tanh, up_proj[g])
        grad_up.append(gelu_pull(matmul(grad_ffn, down_w[g]))[0].astype(jnp.bfloat16))
    up_grad = [contract_rows(normed, grad_up[g]) for g in range(groups)]
    up_b_grad = jnp.stack([jnp.sum(grad_up[g], axis=0, dtype=jnp.float32) for g in range(groups)])
    grad_norm_one = grad_two + sum(contract_cols(grad_up[g], up_w[g]) for g in range(groups))
    gain_one_grad = jnp.sum(grad_norm_one * normal_one, axis=0)
    shift_one_grad = jnp.sum(grad_norm_one, axis=0)
    grad_one = norm_backward(grad_norm_one, normal_one, inverse_one, gain_one)
    grad_attn = grad_one.astype(jnp.bfloat16)
    out_b_grad = jnp.sum(grad_attn, axis=0, dtype=jnp.float32)
    out_grad = [contract_rows(grad_attn, mixture[g]) for g in range(groups)]
    grad_mixture = jnp.stack(
        [matmul(grad_attn, out_w[g]).astype(jnp.bfloat16) for g in range(groups)]
    )
    grad_q, grad_k, grad_v = attend_backward(qkv, seg_row, seg_col, log_total, grad_mixture)
    query_b_grad = jnp.sum(grad_q, axis=1, dtype=jnp.float32)
    value_b_grad = jnp.sum(grad_v, axis=1, dtype=jnp.float32)
    qkv_grad = [
        [contract_rows(tokens, part[g]) for part in (grad_q, grad_k, grad_v)]
        for g in range(groups)
    ]
    grad_tokens = grad_one + sum(
        contract_cols(part[g], qkv_w[g, :, at * heads_width : (at + 1) * heads_width])
        for g in range(groups)
        for at, part in enumerate((grad_q, grad_k, grad_v))
    )

    def rows_of(vector):
        return vector.reshape(dp_size, rows, 1)

    def halves_of(vector):
        return jnp.pad(vector.reshape(dp_size, half, 1), ((0, 0), pad_half, (0, 0)))

    aux_grad = []
    for g in range(groups):
        pieces = [
            rows_of(vector)
            for vector in (
                out_b_grad,
                down_b_grad,
                gain_one_grad,
                shift_one_grad,
                gain_two_grad,
                shift_two_grad,
            )
        ] + [halves_of(query_b_grad[g]), halves_of(value_b_grad[g])]
        pieces.append(jnp.moveaxis(up_b_grad[g].reshape(dp_size, lines, rows), 1, 2))
        piece = jnp.concatenate(pieces, axis=2)
        aux_grad.append(
            jnp.pad(piece, ((0, 0), (0, 0), (0, AUX - piece.shape[2]))).reshape(dp_size * rows, AUX)
        )
    parts = jnp.stack(
        [
            jnp.concatenate(
                [
                    piece.astype(jnp.bfloat16)
                    for piece in (*qkv_grad[g], out_grad[g], up_grad[g], down_grad[g], aux_grad[g])
                ],
                axis=1,
            )
            for g in range(groups)
        ]
    )
    if kernels:
        total = reduce_blocks(parts.reshape(2, 2, 2, 2, 2, rows, columns))
    else:
        total = lax.psum_scatter(
            parts.reshape(groups * dp_size, rows, columns),
            ("tensor", "dp"),
            scatter_dimension=0,
            tiled=False,
        ).astype(jnp.float32)
    small_sum = total[:, at_aux:]
    return (
        block_out,
        grad_tokens,
        total[:, :heads_width],
        total[:, heads_width : 2 * heads_width],
        total[:, 2 * heads_width : at_out],
        total[:, at_out:at_up].T,
        total[:, at_up:at_down],
        total[:, at_down:at_aux].T,
        small_sum[:half, 6],
        small_sum[:half, 7],
        small_sum[:, 0],
        small_sum[:, 8 : 8 + lines].T.reshape(lines * rows),
        small_sum[:, 1],
        small_sum[:, 2],
        small_sum[:, 3],
        small_sum[:, 4],
        small_sum[:, 5],
    )


def solution(mesh):
    return jax.shard_map(
        functools.partial(local, mesh.shape["tensor"], mesh.shape["dp"]),
        mesh=mesh,
        in_specs=(
            P(("dp", "tensor"), None),
            P("dp", None),
            P("dp", "tensor"),
            P("dp", "tensor"),
            P("dp", "tensor"),
            P("tensor", "dp"),
            P("dp", "tensor"),
            P("tensor", "dp"),
            P(("tensor", "dp")),
            P(("tensor", "dp")),
            P("dp"),
            P(("tensor", "dp")),
            P("dp"),
            P("dp"),
            P("dp"),
            P("dp"),
            P("dp"),
            P(("dp", "tensor"), None),
        ),
        out_specs=(
            P(("dp", "tensor"), None),
            P(("dp", "tensor"), None),
            P("dp", "tensor"),
            P("dp", "tensor"),
            P("dp", "tensor"),
            P("tensor", "dp"),
            P("dp", "tensor"),
            P("tensor", "dp"),
            P(("tensor", "dp")),
            P(("tensor", "dp")),
            P("dp"),
            P(("tensor", "dp")),
            P("dp"),
            P("dp"),
            P("dp"),
            P("dp"),
            P("dp"),
        ),
        check_vma=False,
    )
```

time: 1140 us -> 526 us (0.46)
  waiting for transfers between devices: 616 us -> 0 us
  Pallas kernels: 0 us -> 293 us
  blocking collectives: 214 us -> 0 us
  matrix products: 186 us -> 129 us
  between operations: 20.5 us -> 1.97 us
  other arithmetic: 43.7 us -> 28.2 us
    pallas_call x0 -> x4, Pallas kernels: none -> 293 us  [the longest x1 132 us: gather_blocks(): pl.pallas_call(gather_kernel, out_shape=jax.ShapeDtypeStruct((2, 2, 2, 2,...]
    reduce_scatter x7 -> x0, waiting for transfers between devices: 264 us -> none  [the longest x1 77.6 us: local(): lax.psum_scatter(up_grad_w, 'dp', scatter_dimension=0, tiled=True)]
    unnamed x19 -> x0, waiting for transfers between devices: 186 us -> none
    all_gather x6 -> x0, waiting for transfers between devices: 165 us -> none  [the longest x1 44.9 us: local(): shard_rows = lax.all_gather(grad_attn, 'tensor', axis=0, tiled=True)]
    unnamed x2 -> x0, blocking collectives: 125 us -> none
    all_gather x4 -> x0, blocking collectives: 83.9 us -> none  [the longest x1 22.3 us: local(): lax.all_gather(w_key, 'dp', axis=0, tiled=True)]
    dot_general x28 -> x0, matrix products: 73.1 us -> none  [the longest x8 16.9 us: masked_scores(): jnp.einsum('qhe,khe->hqk', queries, key_rows, preferred_element_type=jnp....]
    while x8 -> x0, local copies, waits for them, and re-layouts: 16 us -> none  [the longest x4 9.99 us: local(): lax.map(attend_backward, (queries.reshape(head_shape), key_rows.reshape(h...]
  transfers between devices with their start and end apart: 16 -> 0, of which waited for: 12 -> 0; matrix products, arithmetic and copies ran while one was open for 7% -> 0% of each run, Pallas kernels for 0% -> 0%
where the time goes in v1:
time: 526 us; the launch traced here: 518 us
  Pallas kernels  293 us (56%)
  matrix products  129 us (25%)
  local copies, waits for them, and re-layouts  64.8 us (12%)
  other arithmetic  28.2 us (5%)
    pallas_call x1, Pallas kernels, gather_blocks(): pl.pallas_call(gather_kernel, out_shape=jax.ShapeDtypeStruct((2, 2, 2, 2,...  132 us
    pallas_call x1, Pallas kernels, reduce_blocks(): pl.pallas_call(reduce_kernel, out_shape=jax.ShapeDtypeStruct((rows, colum...  114 us
    dot_general x8, matrix products, matmul(): return jnp.dot(left_rows, right_rows, preferred_element_type=jnp.float32)  46.8 us
    dot_general x12, matrix products, contract_cols(): lax.dot_general(left_rows, right_rows, (((1,), (1,)), ((), ())), preferre...  43.6 us
    dot_general x12, matrix products, contract_rows(): lax.dot_general(left_rows, right_rows, (((0,), (0,)), ((), ())), preferre...  39 us
    pallas_call x1, Pallas kernels, attend_backward(): pl.pallas_call(attend_backward_kernel, grid=(groups, rows // SEQ, pairs),...  29.2 us
    unnamed x104, local copies, waits for them, and re-layouts  27.9 us
    pallas_call x1, Pallas kernels, attend_forward(): pl.pallas_call(attend_forward_kernel, grid=(groups, rows // SEQ, pairs),...  18.3 us

profile of v1, /device:TPU:0, one launch (start us, length us, event | category | flops | bytes accessed | tf_op | source)
XLA Modules:
  0.0 517.7 jit_solution(9820819515967005587)
XLA Ops:
  19.4 132.3 %shard_map.305 = bf16[2,2,2,2,2,48,4736]{6,5,4,3,2,1,0:T(8,128)(2,1)} custom-call(bf16[48,4736]{1,0:T(8,128)(2,1)} %constant_dynamic-update-slice_fusion.own_ref), custom_call_target="tpu_custom_call" | custom-call | tf_op jit(solution)/shard_map/pallas_call | solution.py:121
  155.6 3.7 fusion.19
  159.4 3.7 fusion.20
  163.1 2.6 pad_maximum_fusion.1.q_ref.k_ref.v_ref
  165.7 18.3 %shard_map.306 = (bf16[2,1024,384]{2,1,0:T(8,128)(2,1)}, f32[2,1024,384]{2,1,0:T(8,128)}) custom-call(bf16[2,1024,1152]{2,1,0:T(8,128)(2,1)} %pad_maximum_fusion.1.q_ref.k_ref.v_ref, bf16[2,1024,1152]{2,1,0:T(8,128)(2,1)} %pad_maximum_fusion.1.q_ref.k_ref.v_ref, bf16[2,1024,1152]{2,1,0:T(8,128)(2,1)} %pad_maximum_fusion.1.q_ref.k_ref.v_ref, ...), custom_call_target="tpu_custom_call" | custom-call | tf_op jit(solution)/shard_map/pallas_call | solution.py:298
  184.0 2.5 fusion.62
  186.5 2.2 fusion.87
  189.6 5.0 fusion.31
  194.6 6.2 %fusion.27 = f32[1024,1536]{1,0:T(8,128)S(1)} fusion(bf16[1024,768]{0,1:T(8,128)(2,1)S(1)} %fusion.25, bf16[2,768,4736]{2,1,0:T(8,128)(2,1)} %bitcast.200), kind=kOutput, calls=%fused_computation.65 | convolution fusion | flops 2415919104 | bytes 10223616 | tf_op jit(solution)/shard_map/dot_general | solution.py:29
  200.8 2.7 copy-done.34
  203.4 4.5 fusion.29
  208.0 5.6 %fusion.88 = (f32[1024]{0:T(1024)S(1)}, f32[1024,768]{0,1:T(8,128)S(1)}) fusion(f32[768]{0:T(1024)S(1)} %get-tuple-element.112, f32[1024,768]{0,1:T(8,128)S(1)} %fusion.29, bf16[2,768,4736]{2,1,0:T(8,128)(2,1)} %bitcast.202, f32[1024,1536]{1,0:T(8,128)S(1)} %fusion.31, f32[1536]{0:T(1024)S(1)} %add.194, f32[768]{0:T(1024)S(1)} %get-tuple-element.113, ...), kind=kOutput, calls=%fused_computation.203 | convolution fusion | flops 2437938176 | bytes 18115584 | tf_op jit(solution)/shard_map/dot_general | solution.py:39
  214.0 2.1 copy-done.4
  216.1 2.6 fusion.24
  218.8 2.6 copy.232
  221.4 4.7 fusion.82
  226.2 11.6 %fusion.89 = (bf16[1536]{0:T(1024)(128)(2,1)S(1)}, bf16[1024,1536]{1,0:T(8,128)(2,1)}) fusion(bf16[1024,768]{0,1:T(8,128)(2,1)} %get-tuple-element.125, bf16[2,768,4736]{2,1,0:T(8,128)(2,1)} %bitcast.203, f32[1024,1536]{1,0:T(8,128)} %copy-done.35, f32[1536]{0:T(1024)S(1)} %add.194), kind=kOutput, calls=%fused_computation.204 | convolution fusion | flops 2456812032 | bytes 13378560 | tf_op jit(solution)/shard_map/dot_general | solution.py:29
  237.8 11.8 %fusion.90 = (bf16[1536]{0:T(1024)(128)(2,1)S(1)}, bf16[1024,1536]{1,0:T(8,128)(2,1)}) fusion(bf16[1024,768]{0,1:T(8,128)(2,1)} %get-tuple-element.125, bf16[2,768,4736]{2,1,0:T(8,128)(2,1)} %bitcast.204, f32[1024,1536]{1,0:T(8,128)} %copy-done.34, f32[1536]{0:T(1024)S(1)} %add.189), kind=kOutput, calls=%fused_computation.205 | convolution fusion | flops 2456812032 | bytes 13378560 | tf_op jit(solution)/shard_map/dot_general | solution.py:29
  249.8 5.4 %fusion.26 = f32[1024,768]{0,1:T(8,128)S(1)} fusion(bf16[1024,1536]{1,0:T(8,128)(2,1)} %get-tuple-element.147, bf16[2,768,4736]{2,1,0:T(8,128)(2,1)} %bitcast.205), kind=kOutput, calls=%fused_computation.64 | convolution fusion | flops 2415919104 | bytes 8650752 | tf_op jit(solution)/shard_map/dot_general | solution.py:39
  255.2 7.4 %multiply_reduce_fusion = (bf16[768]{0:T(1024)(128)(2,1)S(1)}, f32[1024]{0:T(1024)S(1)}, f32[1024]{0:T(1024)S(1)}, bf16[768]{0:T(1024)(128)(2,1)S(1)}, f32[1024,768]{0,1:T(8,128)}) fusion(f32[1024,768]{0,1:T(8,128)S(1)} %get-tuple-element.140, f32[1024]{0:T(1024)S(1)} %add_rsqrt_fusion.1, f32[1024]{0:T(1024)S(1)} %broadcast_multiply_fusion.5, ...), kind=kOutput, calls=%fused_computation.45 | convolution fusion | flops 2430857728 | bytes 19702784 | tf_op jit(solution)/shard_map/dot_general | solution.py:39
  262.8 4.2 fusion.84
  267.0 3.4 convolution_convert_fusion.6
  272.1 2.1 copy.217
  276.3 2.7 fusion.35
  282.4 29.2 %shard_map.307 = (bf16[2,1024,384]{2,1,0:T(8,128)(2,1)}, bf16[2,1024,384]{2,1,0:T(8,128)(2,1)}, bf16[2,1024,384]{2,1,0:T(8,128)(2,1)}) custom-call(bf16[2,1024,1152]{2,1,0:T(8,128)(2,1)} %pad_maximum_fusion.1.q_ref.k_ref.v_ref, bf16[2,1024,1152]{2,1,0:T(8,128)(2,1)} %pad_maximum_fusion.1.q_ref.k_ref.v_ref, ...), custom_call_target="tpu_custom_call" | custom-call | tf_op jit(solution)/shard_map/pallas_call | solution.py:314
  319.9 3.3 fusion.37
  323.2 2.2 copy.215
  325.4 3.3 fusion.40
  328.6 2.1 copy.228
  330.8 3.3 fusion.36
  334.0 2.1 copy.214
  336.2 3.3 fusion.39
  341.6 3.3 fusion.38
  344.9 2.1 copy.216
  347.0 3.3 fusion.41
  350.3 2.2 copy.229
  352.5 2.4 fusion.45
  354.9 2.2 fusion.54
  359.2 2.2 fusion.57
  361.4 2.2 fusion.51
  363.7 5.0 add_add_fusion
  368.7 3.7 copy.233
  374.0 4.9 fusion.16
  379.0 3.2 fusion.15
  383.6 2.8 fusion.18
  386.5 3.2 fusion.17
  389.8 5.4 %pad_maximum_fusion.parts_ref = bf16[2,2,2,2,2,48,4736]{6,5,4,3,2,1,0:T(8,128)(2,1)} fusion(bf16[1,2,2,2,2,48,4736]{6,5,4,3,2,1,0:T(8,128)(2,1)S(1)} %bitcast.215, bf16[1,2,2,2,2,48,4736]{6,5,4,3,2,1,0:T(8,128)(2,1)S(1)} %bitcast.216), kind=kLoop, calls=%fused_computation | loop fusion | flops 7274496 | bytes 29097984 | tf_op jit(solution)/shard_map/stack | solution.py:463
  395.2 113.6 %shard_map.308 = f32[48,4736]{1,0:T(8,128)} custom-call(bf16[2,2,2,2,2,48,4736]{6,5,4,3,2,1,0:T(8,128)(2,1)} %pad_maximum_fusion.parts_ref), custom_call_target="tpu_custom_call" | custom-call | tf_op jit(solution)/shard_map/pallas_call | solution.py:211
  (177 shorter events, 55.5 us)
Async XLA Ops:
  0.7 4.2 copy-start
  0.7 15.4 %copy-start.8 = (bf16[1024,768]{1,0:T(8,128)(2,1)S(1)}, bf16[1024,768]{1,0:T(8,128)(2,1)}, u32[]{:S(2)}) copy-start(bf16[1024,768]{1,0:T(8,128)(2,1)} %param.35) | copy-start | bytes 4718596
  0.7 17.1 %copy-start.19 = (bf16[1024,768]{1,0:T(8,128)(2,1)S(1)}, bf16[1024,768]{1,0:T(8,128)(2,1)}, u32[]{:S(2)}) copy-start(bf16[1024,768]{1,0:T(8,128)(2,1)} %param.18) | copy-start | bytes 4718596
  155.2 71.0 %copy-start.32 = (f32[1536]{0:T(1024)}, f32[1536]{0:T(1024)S(1)}, u32[]{:S(2)}) copy-start(f32[1536]{0:T(1024)S(1)} %add.194) | copy-start | bytes 18436
  155.6 82.2 %copy-start.30 = (f32[1536]{0:T(1024)}, f32[1536]{0:T(1024)S(1)}, u32[]{:S(2)}) copy-start(f32[1536]{0:T(1024)S(1)} %add.189) | copy-start | bytes 18436
  184.0 2.5 copy-start.10
  184.0 2.5 copy-start.26
  189.6 5.0 copy-start.20
  194.6 13.4 %copy-start.35 = (f32[1024,1536]{1,0:T(8,128)}, f32[1024,1536]{1,0:T(8,128)S(1)}, u32[]{:S(2)}) copy-start(f32[1024,1536]{1,0:T(8,128)S(1)} %fusion.31) | copy-start | bytes 18874372
  200.8 2.7 copy-start.34
  213.6 5.1 copy-start.2
  213.6 2.5 copy-start.4
  249.8 5.4 %copy-start.3 = (f32[1024,768]{0,1:T(8,128)S(1)}, f32[1024,768]{0,1:T(8,128)}, u32[]{:S(2)}) copy-start(f32[1024,768]{0,1:T(8,128)} %copy-done.2) | copy-start | bytes 9437188
  249.8 5.4 %copy-start.5 = (bf16[1024,768]{0,1:T(8,128)(2,1)S(1)}, bf16[1024,768]{0,1:T(8,128)(2,1)}, u32[]{:S(2)}) copy-start(bf16[1024,768]{0,1:T(8,128)(2,1)} %copy.195) | copy-start | bytes 4718596
  249.8 5.4 %copy-start.37 = (bf16[1024,1536]{1,0:T(8,128)(2,1)S(1)}, bf16[1024,1536]{1,0:T(8,128)(2,1)}, u32[]{:S(2)}) copy-start(bf16[1024,1536]{1,0:T(8,128)(2,1)} %get-tuple-element.145) | copy-start | bytes 9437188
  262.6 4.3 copy-start.28
  267.0 3.4 copy-start.24
  267.0 3.4 copy-start.27
  276.3 2.7 copy-start.25
  352.5 2.4 copy-start.23
  354.9 2.2 copy-start.9
  359.2 2.2 copy-start.7
  361.4 2.3 copy-start.6
  361.4 2.3 copy-start.29
  368.7 3.7 copy-start.17
  368.7 3.8 copy-start.16
  368.7 3.9 copy-start.18
  372.4 1.1 copy-start.12
  372.4 1.6 copy-start.21
  372.4 6.5 %slice-start.2 = ((s8[6291456]{0:T(1024)(128)(4,1)}), s8[4194304]{0:T(1024)(128)(4,1)S(1)}, s32[]{:S(2)}) async-start(s8[6291456]{0:T(1024)(128)(4,1)} %bitcast.229), calls=%async_computation.2 | async-start | bytes 8388608
  374.0 5.0 copy-start.22
  374.0 5.0 copy-start.33
  374.0 5.0 slice-start.3
  379.0 3.4 copy-start.14
  379.0 3.4 copy-start.13
  379.0 4.6 copy-start.36
  382.2 1.1 copy-start.15
  382.2 1.2 copy-start.11
  382.3 4.2 slice-start
  383.6 2.9 copy-start.31
  383.6 2.9 slice-start.1
  395.2 122.1 %copy-start.1 = (s32[4,512]{1,0:T(4,128)S(1)}, s32[4,512]{1,0:T(4,128)}, u32[]{:S(2)}) copy-start(s32[4,512]{1,0:T(4,128)} %param.19) | copy-start | bytes 24580

commit v2 on v1

--- a/solution.py
+++ b/solution.py
@@ -61,8 +61,9 @@
 MESH = pl.DeviceIdType.MESH
 AUX = 128
 KERNEL_VMEM = 56 * 1024 * 1024
-GATHER_ORDERS = ((1, 2, 3, 0, 4), (1, 2, 0, 3, 4))
-REDUCE_ORDERS = tuple(tuple(reversed(order)) for order in GATHER_ORDERS)
+ORDERS = ((1, 2, 0, 3, 4), (1, 2, 3, 0, 4), (1, 2, 3, 0, 4), (1, 2, 0, 3, 4))
+FIRST_TICKS = (0, 2, 0, 2)
+REDUCE_TICKS = (2, 2, 0, 0)
 
 
 def place_bits():
@@ -83,58 +84,60 @@
     pl.semaphore_wait(barrier, 5)
 
 
-def column_halves(columns):
-    first = (columns // 256) * 128 + (128 if (columns // 128) % 2 else 0)
-    return (pl.ds(0, first), pl.ds(first, columns - first)), (first, columns - first)
-
-
-def gather_kernel(own_ref, all_ref, local_sem, send_sem, recv_sem):
+def gather_kernel(*refs):
+    own_refs, all_refs, (local_sem, send_sem, recv_sem) = refs[:4], refs[4:8], refs[8:]
     bits = place_bits()
-    halves, _ = column_halves(own_ref.shape[-1])
-    keep = pltpu.make_async_copy(own_ref, all_ref.at[tuple(bits)], local_sem)
-    keep.start()
+    keeps = [
+        pltpu.make_async_copy(own_refs[chunk], all_refs[chunk].at[tuple(bits)], local_sem.at[chunk])
+        for chunk in range(4)
+    ]
+    for keep in keeps:
+        keep.start()
     meet_partners(bits)
-    keep.wait()
-    pending = [None, None]
-    for step in range(5):
-        for half, order in enumerate(GATHER_ORDERS):
-            if pending[half] is not None:
-                pending[half].wait()
+    for keep in keeps:
+        keep.wait()
+    pending = [None] * 4
+    for tick in range(max(FIRST_TICKS) + 5):
+        for chunk, order in enumerate(ORDERS):
+            step = tick - FIRST_TICKS[chunk]
+            if step < 0 or step > 4:
+                continue
+            if step > 0:
+                pending[chunk].wait()
             done, axis = order[:step], order[step]
             held = tuple(slice(None) if index in done else bits[index] for index in range(5))
-            block = all_ref.at[held + (slice(None), halves[half])]
-            pending[half] = pltpu.make_async_remote_copy(
+            block = all_refs[chunk].at[held]
+            pending[chunk] = pltpu.make_async_remote_copy(
                 src_ref=block,
                 dst_ref=block,
-                send_sem=send_sem.at[half, step],
-                recv_sem=recv_sem.at[half, step],
+                send_sem=send_sem.at[chunk, step],
+                recv_sem=recv_sem.at[chunk, step],
                 device_id=partner(bits, axis),
                 device_id_type=MESH,
             )
-            pending[half].start()
+            pending[chunk].start()
     for copy in pending:
         copy.wait()
 
 
-def gather_blocks(own):
-    rows, columns = own.shape
+def gather_blocks(chunks):
     return pl.pallas_call(
         gather_kernel,
-        out_shape=jax.ShapeDtypeStruct((2, 2, 2, 2, 2, rows, columns), own.dtype),
-        in_specs=[pl.BlockSpec(memory_space=pl.ANY)],
-        out_specs=pl.BlockSpec(memory_space=pl.ANY),
+        out_shape=[jax.ShapeDtypeStruct((2,) * 5 + own.shape, own.dtype) for own in chunks],
+        in_specs=[pl.BlockSpec(memory_space=pl.ANY)] * 4,
+        out_specs=[pl.BlockSpec(memory_space=pl.ANY)] * 4,
         scratch_shapes=[
-            pltpu.SemaphoreType.DMA,
-            pltpu.SemaphoreType.DMA((2, 5)),
-            pltpu.SemaphoreType.DMA((2, 5)),
+            pltpu.SemaphoreType.DMA((4,)),
+            pltpu.SemaphoreType.DMA((4, 5)),
+            pltpu.SemaphoreType.DMA((4, 5)),
         ],
         compiler_params=pltpu.CompilerParams(collective_id=0, has_side_effects=True),
-    )(own)
-
-
-def add_received(bits, order, step, halves, half, own, received):
+    )(*chunks)
+
+
+def add_received(bits, order, step, own, received):
     gone = order[: step + 1]
-    open_axes = [index for index in range(5) if index not in gone and index != 4]
+    open_axes = [index for index in range(4) if index not in gone]
     slices = own.shape[-2] // 16
 
     def one(index, carry):
@@ -144,7 +147,7 @@
         for weight, axis in enumerate(open_axes):
             place[axis] = (code // (2**weight)) % 2
             spot.append(place[axis])
-        target = tuple(place) + (row, halves[half])
+        target = tuple(place) + (row,)
         total = own[target].astype(jnp.float32) + received[tuple(spot) + (row,)].astype(jnp.float32)
         own[target] = total.astype(own.dtype)
         return carry
@@ -152,23 +155,28 @@
     lax.fori_loop(0, slices * 2 ** len(open_axes), one, 0)
 
 
-def reduce_kernel(parts_ref, sum_ref, own, *scratch):
-    received = (scratch[:5], scratch[5:10])
-    local_sem, send_sem, recv_sem = scratch[10:]
+def reduce_kernel(*refs):
+    parts_refs, sum_refs, owns = refs[:4], refs[4:8], refs[8:12]
+    received = [refs[12 + 5 * chunk : 17 + 5 * chunk] for chunk in range(4)]
+    local_sem, send_sem, recv_sem = refs[32:]
     bits = place_bits()
-    halves, _ = column_halves(own.shape[-1])
     everything = slice(None)
-    keep = pltpu.make_async_copy(parts_ref.at[(everything,) * 4 + (bits[4],)], own, local_sem)
-    keep.start()
+    orders = [tuple(reversed(order)) for order in ORDERS]
+    keeps = [
+        pltpu.make_async_copy(
+            parts_refs[chunk].at[(everything,) * 4 + (bits[4],)], owns[chunk], local_sem.at[chunk]
+        )
+        for chunk in range(4)
+    ]
+    for keep in keeps:
+        keep.start()
     meet_partners(bits)
 
-    def copy_of(half, step):
-        order = REDUCE_ORDERS[half]
+    def copy_of(chunk, step):
+        order = orders[chunk]
         axis = order[step]
         if step == 0:
-            block = parts_ref.at[
-                (everything,) * 4 + (1 - bits[4], everything, halves[half])
-            ]
+            block = parts_refs[chunk].at[(everything,) * 4 + (1 - bits[4],)]
         else:
             place = tuple(
                 1 - bits[index]
@@ -176,58 +184,61 @@
                 else (bits[index] if index in order[:step] else everything)
                 for index in range(4)
             )
-            block = own.at[place + (everything, halves[half])]
+            block = owns[chunk].at[place]
         return pltpu.make_async_remote_copy(
             src_ref=block,
-            dst_ref=received[half][step],
-            send_sem=send_sem.at[half, step],
-            recv_sem=recv_sem.at[half, step],
+            dst_ref=received[chunk][step],
+            send_sem=send_sem.at[chunk, step],
+            recv_sem=recv_sem.at[chunk, step],
             device_id=partner(bits, axis),
             device_id_type=MESH,
         )
 
-    pending = [copy_of(half, 0) for half in range(2)]
-    for copy in pending:
-        copy.start()
-    keep.wait()
-    for step in range(5):
-        for half in range(2):
-            pending[half].wait()
-            if step < 4:
+    pending = [None] * 4
+    for tick in range(max(REDUCE_TICKS) + 6):
+        for chunk in range(4):
+            step = tick - REDUCE_TICKS[chunk]
+            if step < 0 or step > 5:
+                continue
+            if step == 0:
+                keeps[chunk].wait()
+            else:
+                pending[chunk].wait()
+            if step == 5:
+                sum_refs[chunk][...] = owns[chunk][tuple(bits[:4])].astype(
+                    jnp.float32
+                ) + received[chunk][4][...].astype(jnp.float32)
+                continue
+            if step > 0:
                 add_received(
-                    bits, REDUCE_ORDERS[half], step, halves, half, own, received[half][step]
+                    bits, orders[chunk], step - 1, owns[chunk], received[chunk][step - 1]
                 )
-                pending[half] = copy_of(half, step + 1)
-                pending[half].start()
-            else:
-                sum_ref[:, halves[half]] = own[tuple(bits[:4]) + (everything, halves[half])].astype(
-                    jnp.float32
-                ) + received[half][4][...].astype(jnp.float32)
-
-
-def reduce_blocks(parts):
-    rows, columns = parts.shape[-2:]
-    _, widths = column_halves(columns)
+            pending[chunk] = copy_of(chunk, step)
+            pending[chunk].start()
+
+
+def reduce_blocks(chunks):
+    blocks = [parts.shape[-2:] for parts in chunks]
     return pl.pallas_call(
         reduce_kernel,
-        out_shape=jax.ShapeDtypeStruct((rows, columns), jnp.float32),
-        in_specs=[pl.BlockSpec(memory_space=pl.ANY)],
-        out_specs=pl.BlockSpec(memory_space=pltpu.VMEM),
-        scratch_shapes=[pltpu.VMEM((2, 2, 2, 2, rows, columns), parts.dtype)]
+        out_shape=[jax.ShapeDtypeStruct(block, jnp.float32) for block in blocks],
+        in_specs=[pl.BlockSpec(memory_space=pl.ANY)] * 4,
+        out_specs=[pl.BlockSpec(memory_space=pltpu.VMEM)] * 4,
+        scratch_shapes=[pltpu.VMEM((2, 2, 2, 2) + block, jnp.bfloat16) for block in blocks]
         + [
-            pltpu.VMEM((2,) * (4 - step) + (rows, width), parts.dtype)
-            for width in widths
+            pltpu.VMEM((2,) * (4 - step) + block, jnp.bfloat16)
+            for block in blocks
             for step in range(5)
         ]
         + [
-            pltpu.SemaphoreType.DMA,
-            pltpu.SemaphoreType.DMA((2, 5)),
-            pltpu.SemaphoreType.DMA((2, 5)),
+            pltpu.SemaphoreType.DMA((4,)),
+            pltpu.SemaphoreType.DMA((4, 5)),
+            pltpu.SemaphoreType.DMA((4, 5)),
         ],
         compiler_params=pltpu.CompilerParams(
             collective_id=1, has_side_effects=True, vmem_limit_bytes=KERNEL_VMEM
         ),
-    )(parts)
+    )(*chunks)
 
 
 def head_scores(query_block, keys, same_doc, lanes, head):
@@ -356,22 +367,21 @@
         axis=1,
     )
     aux = jnp.pad(aux, ((0, 0), (0, AUX - aux.shape[1])))
-    own = jnp.concatenate([w_query, w_key, w_value, w_out.T, w_up, w_down.T, aux], axis=1)
-    columns = own.shape[1]
+    own = (
+        jnp.concatenate([w_query, w_key, w_value], axis=1),
+        jnp.concatenate([w_out.T, aux], axis=1),
+        w_up,
+        w_down.T,
+    )
     if kernels:
         every = gather_blocks(own)
     else:
-        every = lax.all_gather(own, ("tensor", "dp"), axis=0, tiled=False)
-    every = every.reshape(groups, dp_size * rows, columns)
-    at_out = 3 * heads_width
-    at_up = at_out + heads_width
-    at_down = at_up + units
-    at_aux = at_down + units
-    qkv_w = every[:, :, :at_out]
-    out_w = every[:, :, at_out:at_up]
-    up_w = every[:, :, at_up:at_down]
-    down_w = every[:, :, at_down:at_aux]
-    small = every[:, :, at_aux:].astype(jnp.float32)
+        every = [lax.all_gather(chunk, ("tensor", "dp"), axis=0, tiled=False) for chunk in own]
+    qkv_w, out_aux, up_w, down_w = [
+        chunk.reshape(groups, dp_size * rows, chunk.shape[-1]) for chunk in every
+    ]
+    out_w = out_aux[:, :, :heads_width]
+    small = out_aux[:, :, heads_width:].astype(jnp.float32)
     whole = [small[0, :, index] for index in range(6)]
     out_b, down_b, gain_one, shift_one, gain_two, shift_two = whole
     by_device = small.reshape(groups, dp_size, rows, AUX)
@@ -426,15 +436,9 @@
     grad_q, grad_k, grad_v = attend_backward(qkv, seg_row, seg_col, log_total, grad_mixture)
     query_b_grad = jnp.sum(grad_q, axis=1, dtype=jnp.float32)
     value_b_grad = jnp.sum(grad_v, axis=1, dtype=jnp.float32)
-    qkv_grad = [
-        [contract_rows(tokens, part[g]) for part in (grad_q, grad_k, grad_v)]
-        for g in range(groups)
-    ]
-    grad_tokens = grad_one + sum(
-        contract_cols(part[g], qkv_w[g, :, at * heads_width : (at + 1) * heads_width])
-        for g in range(groups)
-        for at, part in enumerate((grad_q, grad_k, grad_v))
-    )
+    grad_qkv = [jnp.concatenate([grad_q[g], grad_k[g], grad_v[g]], axis=1) for g in range(groups)]
+    qkv_grad = [contract_rows(tokens, grad_qkv[g]) for g in range(groups)]
+    grad_tokens = grad_one + sum(contract_cols(grad_qkv[g], qkv_w[g]) for g in range(groups))
 
     def rows_of(vector):
         return vector.reshape(dp_size, rows, 1)
@@ -460,37 +464,37 @@
         aux_grad.append(
             jnp.pad(piece, ((0, 0), (0, 0), (0, AUX - piece.shape[2]))).reshape(dp_size * rows, AUX)
         )
-    parts = jnp.stack(
-        [
-            jnp.concatenate(
-                [
-                    piece.astype(jnp.bfloat16)
-                    for piece in (*qkv_grad[g], out_grad[g], up_grad[g], down_grad[g], aux_grad[g])
-                ],
-                axis=1,
-            )
-            for g in range(groups)
+    out_aux_grad = [
+        jnp.concatenate([out_grad[g].astype(jnp.bfloat16), aux_grad[g].astype(jnp.bfloat16)], axis=1)
+        for g in range(groups)
+    ]
+    parts = [
+        jnp.stack([piece.astype(jnp.bfloat16) for piece in pieces])
+        for pieces in (qkv_grad, out_aux_grad, up_grad, down_grad)
+    ]
+    if kernels:
+        totals = reduce_blocks([part.reshape((2,) * 5 + (rows, part.shape[-1])) for part in parts])
+    else:
+        totals = [
+            lax.psum_scatter(
+                part.reshape(groups * dp_size, rows, part.shape[-1]),
+                ("tensor", "dp"),
+                scatter_dimension=0,
+                tiled=False,
+            ).astype(jnp.float32)
+            for part in parts
         ]
-    )
-    if kernels:
-        total = reduce_blocks(parts.reshape(2, 2, 2, 2, 2, rows, columns))
-    else:
-        total = lax.psum_scatter(
-            parts.reshape(groups * dp_size, rows, columns),
-            ("tensor", "dp"),
-            scatter_dimension=0,
-            tiled=False,
-        ).astype(jnp.float32)
-    small_sum = total[:, at_aux:]
+    qkv_sum, out_aux_sum, up_sum, down_sum = totals
+    small_sum = out_aux_sum[:, heads_width:]
     return (
         block_out,
         grad_tokens,
-        total[:, :heads_width],
-        total[:, heads_width : 2 * heads_width],
-        total[:, 2 * heads_width : at_out],
-        total[:, at_out:at_up].T,
-        total[:, at_up:at_down],
-        total[:, at_down:at_aux].T,
+        qkv_sum[:, :heads_width],
+        qkv_sum[:, heads_width : 2 * heads_width],
+        qkv_sum[:, 2 * heads_width :],
+        out_aux_sum[:, :heads_width].T,
+        up_sum,
+        down_sum.T,
         small_sum[:half, 6],
         small_sum[:half, 7],
         small_sum[:, 0],

time: 526 us -> 471 us (0.90)
  the two profiles are of different devices: /device:TPU:0 before, /device:TPU:7 now
where the time goes in v2:
time: 471 us; the launch traced here: 462 us
  Pallas kernels  276 us (59%)
  matrix products  106 us (23%)
  local copies, waits for them, and re-layouts  51.4 us (11%)
  other arithmetic  26.2 us (6%)
    pallas_call x1, Pallas kernels, gather_blocks(): pl.pallas_call(gather_kernel, out_shape=[jax.ShapeDtypeStruct((2,) * 5 +...  127 us
    pallas_call x1, Pallas kernels, reduce_blocks(): pl.pallas_call(reduce_kernel, out_shape=[jax.ShapeDtypeStruct(block, jnp....  102 us
    dot_general x8, matrix products, matmul(): return jnp.dot(left_rows, right_rows, preferred_element_type=jnp.float32)  49.2 us
    dot_general x8, matrix products, contract_cols(): lax.dot_general(left_rows, right_rows, (((1,), (1,)), ((), ())), preferre...  33.2 us
    pallas_call x1, Pallas kernels, attend_backward(): pl.pallas_call(attend_backward_kernel, grid=(groups, rows // SEQ, pairs),...  28.9 us
    dot_general x8, matrix products, contract_rows(): lax.dot_general(left_rows, right_rows, (((0,), (0,)), ((), ())), preferre...  24 us
    unnamed x150, local copies, waits for them, and re-layouts  22.7 us
    pallas_call x1, Pallas kernels, attend_forward(): pl.pallas_call(attend_forward_kernel, grid=(groups, rows // SEQ, pairs),...  18.1 us

profile of v2, /device:TPU:7, one launch (start us, length us, event | category | flops | bytes accessed | tf_op | source)
XLA Modules:
  0.0 462.0 jit_solution(14680116169532978912)
XLA Ops:
  0.8 2.7 copy.153
  5.2 127.1 %shard_map.305 = (bf16[2,2,2,2,2,48,1152]{6,5,4,3,2,1,0:T(8,128)(2,1)}, bf16[2,2,2,2,2,48,512]{6,5,4,3,2,1,0:T(8,128)(2,1)}, bf16[2,2,2,2,2,48,1536]{6,5,4,3,2,1...) custom-call(bf16[48,1152]{1,0:T(8,128)(2,1)} %pad_maximum_fusion.14.refs_0_, bf16[48,512]{1,0:T(8,128)(2,1)} %fusion.36.refs_1_, ...), custom_call_target="tpu_custom_call" | custom-call | tf_op jit(solution)/shard_map/pallas_call | solution.py:124
  133.3 1.7 slice_reduce_fusion.1
  136.2 3.6 fusion.52
  140.6 3.8 fusion.16
  144.4 2.2 fusion.15
  146.6 2.7 pad_maximum_fusion.q_ref.k_ref.v_ref
  150.9 18.1 %shard_map.306 = (bf16[2,1024,384]{2,1,0:T(8,128)(2,1)}, f32[2,1024,384]{2,1,0:T(8,128)}) custom-call(bf16[2,1024,1152]{2,1,0:T(8,128)(2,1)} %pad_maximum_fusion.q_ref.k_ref.v_ref, bf16[2,1024,1152]{2,1,0:T(8,128)(2,1)} %pad_maximum_fusion.q_ref.k_ref.v_ref, bf16[2,1024,1152]{2,1,0:T(8,128)(2,1)} %pad_maximum_fusion.q_ref.k_ref.v_ref, ...), custom_call_target="tpu_custom_call" | custom-call | tf_op jit(solution)/shard_map/pallas_call | solution.py:309
  169.1 4.1 fusion.28
  174.8 3.9 fusion.55
  179.9 3.4 fusion.50
  183.3 6.2 %multiply_convert_fusion.1 = (bf16[1024,1536]{1,0:T(8,128)(2,1)S(1)}, f32[1024,1536]{1,0:T(8,128)}) fusion(f32[1536]{0:T(1024)S(1)} %copy-done.49, bf16[1024,768]{0,1:T(8,128)(2,1)S(1)} %fusion.21, bf16[768,1536]{1,0:T(8,128)(2,1)S(1)} %bitcast.137), kind=kOutput, calls=%fused_computation.21 | convolution fusion | flops 2431647744 | bytes 13375488 | tf_op jit(solution)/shard_map/dot_general | solution.py:29
  189.6 2.2 fusion.51
  192.0 4.3 fusion.57
  196.2 4.7 %fusion.58 = f32[1024,1536]{1,0:T(8,128)} fusion(bf16[1024,768]{0,1:T(8,128)(2,1)S(1)} %fusion.21, bf16[768,1536]{1,0:T(8,128)(2,1)S(1)} %bitcast.135), kind=kOutput, calls=%fused_computation.152 | convolution fusion | flops 2415919104 | bytes 10223616 | tf_op jit(solution)/shard_map/dot_general | solution.py:29
  202.5 7.8 %fusion.56 = (f32[1024]{0:T(1024)S(1)}, f32[1024,768]{0,1:T(8,128)S(1)}) fusion(f32[768]{0:T(1024)} %get-tuple-element.120, f32[1024,768]{0,1:T(8,128)} %fusion.57, bf16[768,1536]{1,0:T(8,128)(2,1)} %bitcast.139, f32[1024,1536]{1,0:T(8,128)} %fusion.58, f32[1536]{0:T(1024)S(1)} %add.182, f32[768]{0:T(1024)S(1)} %copy-done.47, ...), kind=kOutput, calls=%fused_computation.150 | convolution fusion | flops 2437938176 | bytes 18115584 | tf_op jit(solution)/shard_map/dot_general | solution.py:39
  210.7 2.1 copy-done.4
  212.9 2.6 fusion.20
  215.5 2.6 copy.182
  218.1 3.8 fusion.46
  221.9 21.6 %fusion.42 = (bf16[1536]{0:T(1024)(128)(2,1)S(1)}, bf16[1024,1536]{1,0:T(8,128)(2,1)S(1)}) fusion(f32[1024,1536]{1,0:T(8,128)} %get-tuple-element.171, f32[1536]{0:T(1024)S(1)} %copy-done.50, bf16[1024,768]{0,1:T(8,128)(2,1)S(1)} %get-tuple-element.145, bf16[768,1536]{1,0:T(8,128)(2,1)S(1)} %bitcast.142), kind=kOutput, calls=%fused_computation.140 | convolution fusion | flops 2456812032 | bytes 13378560 | tf_op jit(solution)/shard_map/dot_general | solution.py:29
  243.5 1.6 copy-done.62
  245.1 2.6 fusion.59
  247.8 8.6 %fusion.44 = (bf16[1536]{0:T(1024)(128)(2,1)S(1)}, bf16[1024,1536]{1,0:T(8,128)(2,1)S(1)}) fusion(f32[1024,1536]{1,0:T(8,128)S(1)} %bitcast.172, f32[1536]{0:T(1024)S(1)} %add.182, bf16[1024,768]{0,1:T(8,128)(2,1)S(1)} %get-tuple-element.145, bf16[768,1536]{1,0:T(8,128)(2,1)S(1)} %bitcast.140), kind=kOutput, calls=%fused_computation.141 | convolution fusion | flops 2456812032 | bytes 13378560 | tf_op jit(solution)/shard_map/dot_general | solution.py:29
  256.5 4.1 multiply_reduce_fusion
  265.5 28.9 %shard_map.307 = (bf16[2,1024,384]{2,1,0:T(8,128)(2,1)}, bf16[2,1024,384]{2,1,0:T(8,128)(2,1)}, bf16[2,1024,384]{2,1,0:T(8,128)(2,1)}) custom-call(bf16[2,1024,1152]{2,1,0:T(8,128)(2,1)} %pad_maximum_fusion.q_ref.k_ref.v_ref, bf16[2,1024,1152]{2,1,0:T(8,128)(2,1)} %pad_maximum_fusion.q_ref.k_ref.v_ref, ...), custom_call_target="tpu_custom_call" | custom-call | tf_op jit(solution)/shard_map/pallas_call | solution.py:325
  294.4 1.7 slice_bitcast_fusion.1
  297.0 2.2 copy-done.19
  299.2 2.2 fusion.24
  301.5 4.3 add_add_fusion
  305.8 3.9 copy.183
  309.7 3.6 convolution_convert_fusion.4
  313.4 2.3 convolution_convert_fusion.5
  315.7 2.1 pad_maximum_fusion.3.refs_0_
  318.7 1.8 reduce
  321.7 2.0 convolution_convert_fusion.8
  324.9 2.0 convolution_convert_fusion.9
  329.3 4.9 %convolution_convert_fusion.2 = bf16[768,1536]{1,0:T(8,128)(2,1)S(1)} fusion(bf16[1024,768]{0,1:T(8,128)(2,1)S(1)} %copy-done.25, bf16[1024,1536]{1,0:T(8,128)(2,1)} %copy-done.64), kind=kOutput, calls=%fused_computation.35 | convolution fusion | flops 2417098752 | bytes 7077888 | tf_op jit(solution)/shard_map/dot_general | solution.py:33
  334.2 3.1 convolution_convert_fusion.3
  337.2 2.6 pad_maximum_fusion.1.refs_2_
  339.8 3.3 convolution_convert_fusion
  343.1 2.8 convolution_convert_fusion.1
  346.0 2.6 pad_maximum_fusion.2.refs_3_
  348.5 101.6 %shard_map.308 = (f32[48,1152]{1,0:T(8,128)}, f32[48,512]{1,0:T(8,128)}, f32[48,1536]{1,0:T(8,128)}, f32[48,1536]{1,0:T(8,128)}) custom-call(bf16[2,2,2,2,2,48,1152]{6,5,4,3,2,1,0:T(8,128)(2,1)} %pad_maximum_fusion.3.refs_0_, bf16[2,2,2,2,2,48,512]{6,5,4,3,2,1,0:T(8,128)(2,1)} %pad_maximum_fusion.7.refs_1_, ...), custom_call_target="tpu_custom_call" | custom-call | tf_op jit(solution)/shard_map/pallas_call | solution.py:222
  450.2 1.6 fusion.54
  454.8 1.9 slice_reduce_fusion.8
  458.2 1.7 copy.200
  459.9 1.7 copy.201
  (222 shorter events, 26.9 us)
Async XLA Ops:
  0.7 148.7 %copy-start = (s32[4,512]{1,0:T(4,128)S(1)}, s32[4,512]{1,0:T(4,128)}, u32[]{:S(2)}) copy-start(s32[4,512]{1,0:T(4,128)} %param.19) | copy-start | bytes 24580
  0.7 3.6 copy-start.52
  0.7 3.6 copy-start.53
  0.7 3.6 copy-start.54
  0.7 3.6 copy-start.55
  0.7 3.6 copy-start.56
  0.8 3.6 copy-start.57
  0.8 3.5 copy-start.59
  0.8 3.5 copy-start.51
  0.8 3.4 copy-start.58
  0.8 3.7 copy-start.45
  139.8 4.6 copy-start.16
  140.6 3.8 copy-start.18
  140.6 3.8 copy-start.20
  169.1 4.1 copy-start.21
  179.9 16.4 %copy-start.24 = (bf16[1024,768]{0,1:T(8,128)(2,1)}, bf16[1024,768]{0,1:T(8,128)(2,1)S(1)}, u32[]{:S(2)}) copy-start(bf16[1024,768]{0,1:T(8,128)(2,1)S(1)} %fusion.21) | copy-start | bytes 4718596
  179.9 3.5 copy-start.49
  183.3 6.3 %copy-start.11 = (bf16[1,2,2,2,2,48,1536]{6,5,4,3,2,1,0:T(8,128)(2,1)}, bf16[1,2,2,2,2,48,1536]{6,5,4,3,2,1,0:T(8,128)(2,1)S(1)}, u32[]{:S(2)}) copy-start(bf16[1,2,2,2,2,48,1536]{6,5,4,3,2,1,0:T(8,128)(2,1)S(1)} %get-tuple-element.149) | copy-start | bytes 7077892
  183.3 12.9 %copy-start.9 = (bf16[1,2,2,2,2,48,1536]{6,5,4,3,2,1,0:T(8,128)(2,1)}, bf16[1,2,2,2,2,48,1536]{6,5,4,3,2,1,0:T(8,128)(2,1)S(1)}, u32[]{:S(2)}) copy-start(bf16[1,2,2,2,2,48,1536]{6,5,4,3,2,1,0:T(8,128)(2,1)S(1)} %get-tuple-element.148) | copy-start | bytes 7077892
  183.3 6.3 %slice-start = ((s8[4718592]{0:T(1024)(128)(4,1)}), s8[4194304]{0:T(1024)(128)(4,1)S(1)}, s32[]{:S(2)}) async-start(s8[4718592]{0:T(1024)(128)(4,1)} %bitcast.131), calls=%async_computation | async-start | bytes 8388608
  183.3 6.2 %slice-start.1 = ((s8[4718592]{0:T(1024)(128)(4,1)}), s8[524288]{0:T(1024)(128)(4,1)S(1)}, s32[]{:S(2)}) async-start(s8[4718592]{0:T(1024)(128)(4,1)} %bitcast.131), calls=%async_computation.1 | async-start | bytes 1048576
  191.8 4.4 copy-start.14
  210.3 5.2 %copy-start.2 = (f32[1024,768]{0,1:T(8,128)}, f32[1024,768]{0,1:T(8,128)S(1)}, u32[]{:S(2)}) copy-start(f32[1024,768]{0,1:T(8,128)S(1)} %get-tuple-element.173) | copy-start | bytes 9437188
  218.0 3.8 copy-start.15
  218.0 3.8 copy-start.50
  218.1 29.7 %slice-start.2 = ((s8[6291456]{0:T(1024)(128)(4,1)}), s8[4194304]{0:T(1024)(128)(4,1)S(1)}, s32[]{:S(2)}) async-start(s8[6291456]{0:T(1024)(128)(4,1)} %bitcast.171), calls=%async_computation.2 | async-start | bytes 8388608
  221.8 25.9 %copy-start.26 = (bf16[1024,768]{0,1:T(8,128)(2,1)}, bf16[1024,768]{0,1:T(8,128)(2,1)S(1)}, u32[]{:S(2)}) copy-start(bf16[1024,768]{0,1:T(8,128)(2,1)S(1)} %get-tuple-element.145) | copy-start | bytes 4718596
  221.8 23.3 %copy-start.12 = (bf16[1,2,2,2,2,48,1536]{6,5,4,3,2,1,0:T(8,128)(2,1)S(1)}, bf16[1,2,2,2,2,48,1536]{6,5,4,3,2,1,0:T(8,128)(2,1)}, u32[]{:S(2)}) copy-start(bf16[1,2,2,2,2,48,1536]{6,5,4,3,2,1,0:T(8,128)(2,1)} %copy-done.11) | copy-start | bytes 7077892
  221.9 25.9 %slice-start.3 = ((s8[6291456]{0:T(1024)(128)(4,1)}), s8[2097152]{0:T(1024)(128)(4,1)S(1)}, s32[]{:S(2)}) async-start(s8[6291456]{0:T(1024)(128)(4,1)} %bitcast.171), calls=%async_computation.3 | async-start | bytes 4194304
  247.8 8.7 %copy-start.3 = (f32[1024,768]{0,1:T(8,128)S(1)}, f32[1024,768]{0,1:T(8,128)}, u32[]{:S(2)}) copy-start(f32[1024,768]{0,1:T(8,128)} %copy-done.2) | copy-start | bytes 9437188
  247.8 8.7 %copy-start.5 = (bf16[1024,768]{0,1:T(8,128)(2,1)S(1)}, bf16[1024,768]{0,1:T(8,128)(2,1)}, u32[]{:S(2)}) copy-start(bf16[1024,768]{0,1:T(8,128)(2,1)} %copy.153) | copy-start | bytes 4718596
  247.8 8.7 %copy-start.10 = (bf16[1,2,2,2,2,48,1536]{6,5,4,3,2,1,0:T(8,128)(2,1)S(1)}, bf16[1,2,2,2,2,48,1536]{6,5,4,3,2,1,0:T(8,128)(2,1)}, u32[]{:S(2)}) copy-start(bf16[1,2,2,2,2,48,1536]{6,5,4,3,2,1,0:T(8,128)(2,1)} %copy-done.9) | copy-start | bytes 7077892
  256.5 4.2 copy-start.64
  296.1 5.4 %copy-start.35 = (bf16[1024,384]{1,0:T(8,128)(2,1)}, bf16[1024,384]{1,0:T(8,128)(2,1)S(1)}, u32[]{:S(2)}) copy-start(bf16[1024,384]{1,0:T(8,128)(2,1)S(1)} %get-tuple-element.159) | copy-start | bytes 2359300
  296.4 5.0 %copy-start.33 = (bf16[1024,384]{1,0:T(8,128)(2,1)}, bf16[1024,384]{1,0:T(8,128)(2,1)S(1)}, u32[]{:S(2)}) copy-start(bf16[1024,384]{1,0:T(8,128)(2,1)S(1)} %get-tuple-element.158) | copy-start | bytes 2359300
  296.4 5.0 %copy-start.37 = (bf16[1024,384]{1,0:T(8,128)(2,1)}, bf16[1024,384]{1,0:T(8,128)(2,1)S(1)}, u32[]{:S(2)}) copy-start(bf16[1024,384]{1,0:T(8,128)(2,1)S(1)} %get-tuple-element.157) | copy-start | bytes 2359300
  296.9 4.5 copy-start.39
  296.9 4.5 copy-start.41
  305.7 3.9 copy-start.22
  305.7 3.9 copy-start.36
  305.8 3.9 copy-start.38
  309.7 3.7 copy-start.32
  309.7 3.7 copy-start.34
  309.7 3.7 copy-start.40
  329.3 4.9 %copy-start.63 = (bf16[1024,1536]{1,0:T(8,128)(2,1)S(1)}, bf16[1024,1536]{1,0:T(8,128)(2,1)}, u32[]{:S(2)}) copy-start(bf16[1024,1536]{1,0:T(8,128)(2,1)} %copy-done.62) | copy-start | bytes 9437188
  329.3 10.6 %slice-start.4 = ((s8[6291456]{0:T(1024)(128)(4,1)}), s8[4194304]{0:T(1024)(128)(4,1)S(1)}, s32[]{:S(2)}) async-start(s8[6291456]{0:T(1024)(128)(4,1)} %bitcast.173), calls=%async_computation.4 | async-start | bytes 8388608
  334.1 5.7 %slice-start.5 = ((s8[6291456]{0:T(1024)(128)(4,1)}), s8[2097152]{0:T(1024)(128)(4,1)S(1)}, s32[]{:S(2)}) async-start(s8[6291456]{0:T(1024)(128)(4,1)} %bitcast.173), calls=%async_computation.5 | async-start | bytes 4194304
  348.5 113.0 %copy-start.1 = (s32[4,512]{1,0:T(4,128)S(1)}, s32[4,512]{1,0:T(4,128)}, u32[]{:S(2)}) copy-start(s32[4,512]{1,0:T(4,128)} %param.19) | copy-start | bytes 24580
  (23 other events, 52.9 us)
